TPU v7x, 128 devices: a whole 4x4x4 slice. The times are simulated.
128 devices in a mesh: gy: 8 (over y_hi, x), gz: 16 (over y_lo, z, core).
Axes of the slice: x: 4, y: 4 (y_hi: 2, y_lo: 2; y = y_hi * 2 + y_lo), z: 4, core: 2. Of those that a mesh axis runs over, the one named last changes fastest.
Arguments:
- kspace: bfloat16 [2, 16, 64, 512, 128], P(None, None, 'gz', 'gy'), may hold values from -6 to 6
- measured: bfloat16 [2, 16, 64, 512, 128], P(None, None, 'gz', 'gy'), may hold values from -6 to 6
- sample_mask: int32 [64, 512], P('gz', 'gy'), may hold values 0 or 1
- step_size: float32 [1], replicated, may hold values from 0.3 to 1
- coil_field: bfloat16 [2, 128, 16, 64, 512], P(None, ('gy', 'gz')), may hold values from -1 to 1
- conv_in: bfloat16 [32, 2, 3, 3, 3], replicated, may hold values from -0.875 to 0.875
- bias_in: float32 [32], replicated, may hold values from -3 to 3
- conv_out: bfloat16 [2, 32, 3, 3, 3], replicated, may hold values from -0.5 to 0.5
- cotangent: bfloat16 [2, 16, 64, 512, 128], P(None, None, 'gz', 'gy'), may hold values from -6 to 6
Outputs:
- kspace_next: bfloat16 [2, 16, 64, 512, 128], P(None, None, 'gz', 'gy')
- grad_conv_in: float32 [32, 2, 3, 3, 3], replicated
- grad_bias_in: float32 [32], replicated
- grad_conv_out: float32 [2, 32, 3, 3, 3], replicated
All inputs are finite; a program needn't handle non-finite values. No bound on the sum of `sample_mask` on one device may be relied on, other than what follows from the above.
Results may differ from a plain program's by a relative error of at most 0.012.
Values may be sent and summed in bfloat16 or wider, within the bound.
A program may use at most 256 MiB of HBM per device.

v0:
```python
import math

import jax
import jax.numpy as jnp
from jax import lax
from jax.sharding import PartitionSpec as P


def with_halo(cells, sides, width):
    for axis, dim in sides:
        count = lax.axis_size(axis)
        ends = count - 1
        head = lax.slice_in_dim(cells, 0, width, axis=dim)
        tail = lax.slice_in_dim(cells, cells.shape[dim] - width, cells.shape[dim], axis=dim)
        cells = jnp.concatenate(
            [
                lax.ppermute(tail, axis, [(i, (i + 1) % count) for i in range(ends)]),
                cells,
                lax.ppermute(head, axis, [((i + 1) % count, i) for i in range(ends)]),
            ],
            axis=dim,
        )
    return cells


def dft_tables(length):
    index_range = jnp.arange(length, dtype=jnp.int32)
    phase_index = index_range[:, None] * index_range[None, :] % length
    angle_table = phase_index.astype(jnp.float32) * (2.0 * math.pi / length)
    factor = 1.0 / math.sqrt(length)
    return (
        (jnp.cos(angle_table) * factor).astype(jnp.bfloat16),
        (jnp.sin(angle_table) * factor).astype(jnp.bfloat16),
    )


def transform(spectrum, formula, tables, inverse):
    cosine = jnp.einsum(formula, spectrum, tables[0], preferred_element_type=jnp.float32)
    sine_part = jnp.einsum(formula, spectrum, tables[1], preferred_element_type=jnp.float32)
    if inverse:
        real_part = cosine[0] - sine_part[1]
        imag_part = cosine[1] + sine_part[0]
    else:
        real_part = cosine[0] + sine_part[1]
        imag_part = cosine[1] - sine_part[0]
    return jnp.stack([real_part, imag_part])


def combine_coils(coil_images, coil_field):
    sens_real = coil_field[0].astype(jnp.float32)
    sens_imag = coil_field[1].astype(jnp.float32)
    real_part = jnp.sum(sens_real * coil_images[0] + sens_imag * coil_images[1], axis=1)
    imag_part = jnp.sum(sens_real * coil_images[1] - sens_imag * coil_images[0], axis=1)
    return jnp.stack([real_part, imag_part]).astype(jnp.bfloat16)


def columns(padded, depth_span, row_span, x_span, flipped):
    pieces = []
    for shift_z in range(3):
        for shift_y in range(3):
            for shift_x in range(3):
                anchor_z = 2 - shift_z if flipped else shift_z
                anchor_y = 2 - shift_y if flipped else shift_y
                anchor_x = 2 - shift_x if flipped else shift_x
                pieces.append(
                    padded[
                        :,
                        anchor_z : anchor_z + depth_span,
                        anchor_y : anchor_y + row_span,
                        anchor_x : anchor_x + x_span,
                    ]
                )
    stacked = jnp.stack(pieces)
    return stacked.reshape(stacked.shape[0] * stacked.shape[1], depth_span * row_span * x_span)


def pad_width(volume, amount):
    return jnp.pad(volume, ((0, 0), (0, 0), (0, 0), (amount, amount)))


def on_device(
    kspace, measured, sample_mask, step_size, coil_field, conv_in, bias_in, conv_out, cotangent
):
    count_y = lax.axis_size("gy")
    count_z = lax.axis_size("gz")
    all_tiles = count_y * count_z
    coil_count = kspace.shape[1]
    depth_tile = kspace.shape[2]
    row_tile = kspace.shape[3]
    x_cells = kspace.shape[4]
    slices_dev = coil_field.shape[1]
    channels = conv_in.shape[0]
    length_y = row_tile * count_y
    length_z = depth_tile * count_z
    tables_y = dft_tables(length_y)
    tables_z = dft_tables(length_z)
    split_y = tuple((one_table.reshape(count_y, row_tile, length_y) for one_table in tables_y))
    split_z = tuple((one_table.reshape(count_z, depth_tile, length_z) for one_table in tables_z))
    outer_y = tuple((one_table.reshape(length_y, count_y, row_tile) for one_table in tables_y))
    outer_z = tuple((one_table.reshape(length_z, count_z, depth_tile) for one_table in tables_z))

    def to_slices(spectrum):
        leading = spectrum.transpose(0, 4, 1, 2, 3)
        stacked = leading.reshape(2, all_tiles, slices_dev, coil_count, depth_tile, row_tile)
        tile_data = lax.all_to_all(stacked, ("gy", "gz"), split_axis=1, concat_axis=1, tiled=True)
        tile_data = tile_data.reshape(
            2, count_y, count_z, slices_dev, coil_count, depth_tile, row_tile
        )
        partial_y = transform(tile_data, "pabxczy,ayY->pbxczY", split_y, True).astype(jnp.bfloat16)
        return transform(partial_y, "pbxczY,bzZ->pxcZY", split_z, True)

    def to_tiles(slice_image):
        tile_parts = slice_image.reshape(2, slices_dev, count_z, depth_tile, count_y, row_tile)
        tile_parts = tile_parts.transpose(0, 4, 2, 1, 3, 5).reshape(
            2, all_tiles, slices_dev, depth_tile, row_tile
        )
        received = lax.all_to_all(tile_parts, ("gy", "gz"), split_axis=1, concat_axis=1, tiled=True)
        return received.reshape(2, x_cells, depth_tile, row_tile).transpose(0, 2, 3, 1)

    image_field = to_tiles(combine_coils(to_slices(kspace), coil_field))
    kernel_in = conv_in.transpose(0, 2, 3, 4, 1).reshape(channels, 27 * 2)
    padded = pad_width(with_halo(image_field, (("gy", 2), ("gz", 1)), 1), 1)
    image_cols = columns(padded, depth_tile, row_tile, x_cells, False)
    pre_act = jnp.dot(kernel_in, image_cols, preferred_element_type=jnp.float32) + bias_in[:, None]
    hidden = (
        jax.nn.silu(pre_act).astype(jnp.bfloat16).reshape(channels, depth_tile, row_tile, x_cells)
    )
    hidden_pad = pad_width(with_halo(hidden, (("gy", 2), ("gz", 1)), 1), 1)
    kernel_out = conv_out.transpose(2, 3, 4, 0, 1).reshape(27 * 2, channels)
    products = jnp.dot(
        kernel_out, hidden_pad.reshape(channels, -1), preferred_element_type=jnp.float32
    )
    products = products.reshape(27, 2, depth_tile + 2, row_tile + 2, x_cells + 2)
    refine_sum = jnp.zeros((2, depth_tile, row_tile, x_cells), jnp.float32)
    for shift_z in range(3):
        for shift_y in range(3):
            for shift_x in range(3):
                offset = shift_z * 9 + shift_y * 3 + shift_x
                refine_sum = (
                    refine_sum
                    + products[
                        offset,
                        :,
                        shift_z : shift_z + depth_tile,
                        shift_y : shift_y + row_tile,
                        shift_x : shift_x + x_cells,
                    ]
                )
    refine_image = refine_sum.astype(jnp.bfloat16)
    outgoing = refine_image.transpose(0, 3, 1, 2).reshape(
        2, all_tiles, slices_dev, depth_tile, row_tile
    )
    received = lax.all_to_all(outgoing, ("gy", "gz"), split_axis=1, concat_axis=1, tiled=True)
    received = received.reshape(2, count_y, count_z, slices_dev, depth_tile, row_tile)
    refine_slab = received.transpose(0, 3, 2, 4, 1, 5).reshape(2, slices_dev, length_z, length_y)
    sens_real = coil_field[0].astype(jnp.float32)
    sens_imag = coil_field[1].astype(jnp.float32)
    refine_real = refine_slab[0].astype(jnp.float32)[:, None]
    refine_imag = refine_slab[1].astype(jnp.float32)[:, None]
    coil_refine = jnp.stack(
        [
            sens_real * refine_real - sens_imag * refine_imag,
            sens_real * refine_imag + sens_imag * refine_real,
        ]
    ).astype(jnp.bfloat16)
    partial_z = transform(coil_refine, "pxcZY,Zbz->pbxczY", outer_z, False).astype(jnp.bfloat16)
    final_y = transform(partial_z, "pbxczY,Yay->pabxczy", outer_y, False).astype(jnp.bfloat16)
    final_y = final_y.reshape(2, all_tiles, slices_dev, coil_count, depth_tile, row_tile)
    refine = lax.all_to_all(final_y, ("gy", "gz"), split_axis=1, concat_axis=1, tiled=True)
    refine = refine.reshape(2, x_cells, coil_count, depth_tile, row_tile).transpose(0, 2, 3, 4, 1)
    weight = sample_mask.astype(jnp.float32)[None, None, :, :, None]
    current = kspace.astype(jnp.float32)
    kspace_next = (
        current
        - step_size[0] * weight * (current - measured.astype(jnp.float32))
        + refine.astype(jnp.float32)
    ).astype(jnp.bfloat16)
    grad_image = to_tiles(combine_coils(to_slices(cotangent), coil_field))
    grad_pad = pad_width(with_halo(grad_image, (("gy", 2), ("gz", 1)), 1), 1)
    grad_cols = columns(grad_pad, depth_tile, row_tile, x_cells, True)
    kernel_back = conv_out.transpose(1, 2, 3, 4, 0).reshape(channels, 27 * 2)
    back_hidden = jnp.dot(kernel_back, grad_cols, preferred_element_type=jnp.float32)
    sigmoid_pre = jax.nn.sigmoid(pre_act)
    back_pre = (back_hidden * sigmoid_pre * (1.0 + pre_act * (1.0 - sigmoid_pre))).astype(
        jnp.bfloat16
    )
    grad_in = jnp.einsum("fn,kn->fk", back_pre, image_cols, preferred_element_type=jnp.float32)
    grad_in = grad_in.reshape(channels, 3, 3, 3, 2).transpose(0, 4, 1, 2, 3)
    grad_bias = jnp.sum(back_pre, axis=1, dtype=jnp.float32)
    grad_big = jnp.pad(grad_image, ((0, 0), (2, 2), (2, 2), (2, 2)))
    grad_cols_wide = columns(grad_big, depth_tile + 2, row_tile + 2, x_cells + 2, True)
    grad_out = jnp.einsum(
        "fn,kn->fk",
        hidden_pad.reshape(channels, -1),
        grad_cols_wide,
        preferred_element_type=jnp.float32,
    )
    grad_out = grad_out.reshape(channels, 3, 3, 3, 2).transpose(4, 0, 1, 2, 3)
    totals = lax.psum((grad_in, grad_bias, grad_out), ("gy", "gz"))
    norm_factor = 1.0 / math.sqrt(x_cells * length_y * length_z)
    return (kspace_next, totals[0] * norm_factor, totals[1] * norm_factor, totals[2] * norm_factor)


def solution(mesh):
    in_specs = (
        P(None, None, "gz", "gy", None),
        P(None, None, "gz", "gy", None),
        P("gz", "gy"),
        P(),
        P(None, ("gy", "gz"), None, None, None),
        P(),
        P(),
        P(),
        P(None, None, "gz", "gy", None),
    )
    out_specs = (P(None, None, "gz", "gy", None), P(), P(), P())
    return jax.shard_map(
        on_device, mesh=mesh, in_specs=in_specs, out_specs=out_specs, check_vma=False
    )
```

profile of v0, /device:TPU:1, one launch (start us, length us, event | category | flops | bytes accessed | tf_op | source)
XLA Modules:
  0.0 652.7 jit_solution(3019155422959473613)
XLA Ops:
  0.6 7.5 %copy.233 = bf16[2,16,4,64,128]{3,1,2,0,4:T(8,128)(2,1)} copy(bf16[2,16,4,64,128]{4,3,2,1,0:T(8,128)(2,1)} %param.9) | data formatting | bytes 4194304 | tf_op args[0]
  8.1 6.0 bitcast_bitcast_fusion.1
  14.1 7.8 %reshape.850 = bf16[128,2,4096]{2,1,0:T(2,128)(2,1)} reshape(bf16[128,1,2,4,16,64]{5,4,3,2,1,0:T(8,128)(2,1)} %bitcast_bitcast_fusion.1) | data formatting | bytes 4194304
  21.9 12.0 %all-to-all-start = ((bf16[128,2,4096]{2,1,0:T(2,128)(2,1)}), bf16[128,2,4096]{2,1,0:T(2,128)(2,1)}, u32[]{:S(2)}, u32[]{:S(2)}) async-start(bf16[128,2,4096]{2,1,0:T(2,128)(2,1)} %reshape.850), calls=%async_computation | async-start | bytes 4194304 | tf_op jit(solution)/shard_map/all_to_all | solution.py:105
  33.9 5.4 copy.230
  40.5 7.5 %copy.263 = bf16[2,16,4,64,128]{3,1,2,0,4:T(8,128)(2,1)} copy(bf16[2,16,4,64,128]{4,3,2,1,0:T(8,128)(2,1)} %param.17) | data formatting | bytes 4194304 | tf_op args[8]
  48.0 6.0 bitcast_bitcast_fusion
  54.0 7.8 %reshape.858 = bf16[128,2,4096]{2,1,0:T(2,128)(2,1)} reshape(bf16[128,1,2,4,16,64]{5,4,3,2,1,0:T(8,128)(2,1)} %bitcast_bitcast_fusion) | data formatting | bytes 4194304
  62.4 5.5 copy.231
  68.5 9.8 %all-to-all-start.4 = ((bf16[128,2,4096]{2,1,0:T(2,128)(2,1)}), bf16[128,2,4096]{2,1,0:T(2,128)(2,1)S(1)}, u32[]{:S(2)}, u32[]{:S(2)}) async-start(bf16[128,2,4096]{2,1,0:T(2,128)(2,1)} %reshape.858), calls=%async_computation.4 | async-start | bytes 4194304 | tf_op jit(solution)/shard_map/all_to_all | solution.py:105
  78.3 8.1 %reshape.851 = bf16[128,1,2,4,16,64]{5,4,3,2,1,0:T(8,128)(2,1)} reshape(bf16[128,2,4096]{2,1,0:T(2,128)(2,1)} %all-to-all-done) | data formatting | bytes 4194304
  86.4 7.6 %fusion.24 = f32[2,16,16,4,512]{4,2,3,1,0:T(8,128)S(1)} fusion(s32[8,64]{1,0:T(8,128)S(1)} %multiply_add_fusion, bf16[2,8,16,16,4,64]{5,3,4,0,2,1:T(8,128)(2,1)} %bitcast.749), kind=kOutput, calls=%fused_computation.77 | convolution fusion | flops 1077936128 | bytes 6293504 | tf_op jit(solution)/shard_map/pabxczy,ayY->pbxczY/dot_general | solution.py:38
  94.0 5.3 fusion.27
  100.6 11.2 %pad_maximum_fusion.2 = bf16[2,16,16,4,512]{4,2,3,1,0:T(8,128)(2,1)S(1)} fusion(bf16[1,16,16,4,512]{4,2,3,1,0:T(8,128)(2,1)S(1)} %get-tuple-element.40, bf16[1,16,16,4,512]{4,2,3,1,0:T(8,128)(2,1)S(1)} %get-tuple-element.39), kind=kLoop, calls=%fused_computation.119 | loop fusion | flops 1048576 | bytes 4194304 | tf_op jit(solution)/shard_map/stack | solution.py:46
  111.8 3.0 convolution_bitcast_fusion.9
  114.8 3.0 convolution_bitcast_fusion.8
  120.5 9.8 %all-to-all-start.1 = ((bf16[128,2,256]{2,1,0:T(2,128)(2,1)}), bf16[128,2,256]{2,1,0:T(2,128)(2,1)S(1)}, u32[]{:S(2)}, u32[]{:S(2)}) async-start(bf16[128,2,256]{2,1,0:T(2,128)(2,1)} %reshape.852), calls=%async_computation.1 | async-start | bytes 262144 | tf_op jit(solution)/shard_map/all_to_all | solution.py:117
  130.9 4.1 reshape.859
  135.0 5.5 all-to-all-done.1
  141.1 2.2 collective-permute-start
  144.6 9.6 %fusion.30 = f32[2,16,16,4,512]{4,2,3,1,0:T(8,128)} fusion(s32[8,64]{1,0:T(8,128)S(1)} %multiply_add_fusion, bf16[2,8,16,16,4,64]{5,3,4,0,2,1:T(8,128)(2,1)} %bitcast.747), kind=kOutput, calls=%fused_computation.79 | convolution fusion | flops 1077936128 | bytes 6293504 | tf_op jit(solution)/shard_map/pabxczy,ayY->pbxczY/dot_general | solution.py:38
  155.0 3.1 collective-permute-start.2
  158.1 2.3 collective-permute-start.3
  160.4 7.3 %fusion.33 = f32[2,16,16,4,512]{4,2,3,1,0:T(8,128)} fusion(s32[8,64]{1,0:T(8,128)S(1)} %multiply_add_fusion, bf16[2,8,16,16,4,64]{5,3,4,0,2,1:T(8,128)(2,1)S(1)} %bitcast.748), kind=kOutput, calls=%fused_computation.80 | convolution fusion | flops 1077936128 | bytes 6293504 | tf_op jit(solution)/shard_map/pabxczy,ayY->pbxczY/dot_general | solution.py:39
  195.3 10.1 %copy.242 = bf16[27,2,4,64,128]{4,3,2,1,0:T(8,128)(2,1)S(1)} copy(bf16[27,2,4,64,128]{3,2,1,4,0:T(4,128)(2,1)} %fusion.209) | data formatting | bytes 7077888 | tf_op jit(solution)/shard_map/stack | solution.py:73
  205.4 3.5 reshape.799
  209.0 2.8 fusion.2
  214.0 4.5 collective-permute-start.4
  222.7 1.8 collective-permute-done.5
  224.7 5.1 collective-permute-start.6
  229.8 2.1 collective-permute-start.7
  233.5 5.0 convolution_bitcast_fusion.4
  238.4 2.1 collective-permute-done.7
  242.2 5.6 pad.16.clone
  247.8 9.9 %reshape.802 = bf16[32,51480]{1,0:T(8,128)(2,1)} reshape(bf16[32,6,66,130]{3,2,1,0:T(8,128)(2,1)} %pad.16.clone) | data formatting | bytes 6589440 | tf_op jit(solution)/shard_map/reshape | solution.py:131
  257.6 7.8 %convolution_bitcast_fusion = f32[54,51480]{1,0:T(8,128)} fusion(bf16[32,51480]{1,0:T(8,128)(2,1)} %reshape.802, bf16[54,32]{1,0:T(8,128)(2,1)} %reshape.803), kind=kOutput, calls=%fused_computation | convolution fusion | flops 177914880 | bytes 14417856 | tf_op jit(solution)/shard_map/dot_general | solution.py:130
  265.4 19.2 %reshape.804 = f32[27,2,6,66,130]{4,3,2,1,0:T(8,128)} reshape(f32[54,51480]{1,0:T(8,128)} %convolution_bitcast_fusion) | data formatting | bytes 22239360 | tf_op jit(solution)/shard_map/reshape | solution.py:133
  284.6 6.7 %fusion.237 = bf16[2,128,1,4,64]{1,4,3,0,2:T(8,128)(2,1)} fusion(f32[27,2,6,66,130]{4,3,2,1,0:T(8,128)} %reshape.804), kind=kLoop, calls=%fused_computation.398 | loop fusion | flops 1769472 | bytes 7208960 | tf_op jit(solution)/shard_map/reshape | solution.py:150
  294.9 18.5 %all-to-all-start.2 = ((bf16[128,2,256]{2,1,0:T(2,128)(2,1)}), bf16[128,2,256]{2,1,0:T(2,128)(2,1)}, u32[]{:S(2)}, u32[]{:S(2)}) async-start(bf16[128,2,256]{2,1,0:T(2,128)(2,1)} %reshape.854), calls=%async_computation.2 | async-start | bytes 262144 | tf_op jit(solution)/shard_map/all_to_all | solution.py:153
  313.4 6.5 %convolution_bitcast_fusion.5 = f32[2,1,16,64,512]{4,3,2,0,1:T(8,128)} fusion(bf16[2,16,16,4,512]{4,2,3,1,0:T(8,128)(2,1)} %copy-done.1, s32[16,4]{0,1:T(4,128)S(1)} %multiply_add_fusion.1), kind=kOutput, calls=%fused_computation.82 | convolution fusion | flops 134283264 | bytes 6291712 | tf_op jit(solution)/shard_map/pbxczY,bzZ->pxcZY/dot_general | solution.py:38
  320.0 2.6 dot_general.112
  322.6 9.5 %reshape.848 = bf16[32,51480,1,1,1]{1,0,2,3,4:T(8,128)(2,1)} reshape(bf16[32,6,66,130]{3,2,1,0:T(8,128)(2,1)} %pad.16.clone) | data formatting | bytes 6589440 | tf_op jit(solution)/shard_map/reshape | solution.py:131
  334.3 4.7 fusion.48
  342.3 9.6 %convolution_bitcast_fusion.3 = f32[2,8,16,1,16,4,64]{6,4,5,2,0,1,3:T(8,128)} fusion(bf16[2,16,16,4,512]{4,1,2,3,0:T(8,128)(2,1)S(1)} %pad_maximum_fusion.4, s32[8,64]{1,0:T(8,128)S(1)} %multiply_add_fusion), kind=kOutput, calls=%fused_computation.47 | convolution fusion | flops 1077936128 | bytes 6293504 | tf_op jit(solution)/shard_map/pbxczY,Yay->pabxczy/dot_general | solution.py:38
  351.9 9.5 %convolution_bitcast_fusion.2 = f32[2,8,16,1,16,4,64]{6,4,5,2,0,1,3:T(8,128)} fusion(bf16[2,16,16,4,512]{4,1,2,3,0:T(8,128)(2,1)S(1)} %pad_maximum_fusion.4, s32[8,64]{1,0:T(8,128)S(1)} %multiply_add_fusion), kind=kOutput, calls=%fused_computation.46 | convolution fusion | flops 1077936128 | bytes 6293504 | tf_op jit(solution)/shard_map/pbxczY,Yay->pabxczy/dot_general | solution.py:39
  362.8 10.3 %all-to-all-start.5 = ((bf16[128,2,256]{2,1,0:T(2,128)(2,1)}), bf16[128,2,256]{2,1,0:T(2,128)(2,1)S(1)}, u32[]{:S(2)}, u32[]{:S(2)}) async-start(bf16[128,2,256]{2,1,0:T(2,128)(2,1)} %reshape.860), calls=%async_computation.5 | async-start | bytes 262144 | tf_op jit(solution)/shard_map/all_to_all | solution.py:117
  373.1 6.9 %fusion.12 = (bf16[1,8,16,1,16,4,64]{6,4,5,2,0,1,3:T(8,128)(2,1)S(1)}, bf16[1,8,16,1,16,4,64]{6,4,5,2,0,1,3:T(8,128)(2,1)S(1)}) fusion(f32[2,8,16,1,16,4,64]{6,4,5,2,0,1,3:T(8,128)} %convolution_bitcast_fusion.2, f32[2,8,16,1,16,4,64]{6,4,5,2,0,1,3:T(8,128)} %convolution_bitcast_fusion.3), kind=kLoop, calls=%fused_computation.26 | loop fusion | flops 2097152 | bytes 10485760 | tf_op jit(solution)/shard_map/convert.13
  382.5 5.3 fusion.332
  387.7 8.5 %reshape.856 = bf16[128,2,4096]{2,1,0:T(2,128)(2,1)} reshape(bf16[128,1,2,16,4,64]{5,4,3,2,1,0:T(4,128)(2,1)} %fusion.332) | data formatting | bytes 4194304
  396.3 10.6 %all-to-all-start.3 = ((bf16[128,2,4096]{2,1,0:T(2,128)(2,1)}), bf16[128,2,4096]{2,1,0:T(2,128)(2,1)}, u32[]{:S(2)}, u32[]{:S(2)}) async-start(bf16[128,2,4096]{2,1,0:T(2,128)(2,1)} %reshape.856), calls=%async_computation.3 | async-start | bytes 4194304 | tf_op jit(solution)/shard_map/all_to_all | solution.py:169
  435.2 3.3 collective-permute-start.8
  441.0 18.6 %copy.274 = bf16[27,2,6,66,130]{4,3,2,1,0:T(8,128)(2,1)} copy(bf16[27,2,6,66,130]{3,2,1,4,0:T(8,128)(2,1)} %fusion.149) | data formatting | bytes 11119680 | tf_op jit(solution)/shard_map/stack | solution.py:73
  459.6 28.0 %dot_general.114 = bf16[3,3,3,2,51480]{4,3,2,1,0:T(2,128)(2,1)} reshape(bf16[27,2,6,66,130]{4,3,2,1,0:T(8,128)(2,1)} %copy.274) | data formatting | bytes 11119680 | tf_op jit(solution)/shard_map/fn,kn->fk/dot_general | solution.py:192
  488.4 3.8 collective-permute-start.10
  492.2 2.1 collective-permute-start.11
  494.3 8.2 %fusion.74 = f32[2,32,3,3,3]{1,4,0,3,2:T(4,128)} fusion(bf16[3,3,3,2,51480]{4,3,2,1,0:T(2,128)(2,1)} %dot_general.114, bf16[32,51480,1,1,1]{1,0,2,3,4:T(8,128)(2,1)} %reshape.848), kind=kOutput, calls=%fused_computation.144 | convolution fusion | flops 177914880 | bytes 8861472 | tf_op jit(solution)/shard_map/fn,kn->fk/dot_general | solution.py:192
  530.1 10.1 %copy.271 = bf16[27,2,4,64,128]{4,3,2,1,0:T(8,128)(2,1)S(1)} copy(bf16[27,2,4,64,128]{3,2,1,4,0:T(4,128)(2,1)} %fusion.169) | data formatting | bytes 7077888 | tf_op jit(solution)/shard_map/stack | solution.py:73
  540.3 3.5 reshape.811
  543.8 5.7 convert_reduce_fusion
  549.5 2.6 fusion.69
  552.1 71.1 %all-reduce.4 = (f32[32,2,3,3,3]{0,4,1,3,2:T(4,128)S(1)}, f32[32]{0:T(128)S(1)}, f32[2,32,3,3,3]{1,4,0,3,2:T(4,128)S(1)}) all-reduce(f32[32,2,3,3,3]{0,4,1,3,2:T(4,128)S(1)} %fusion.69, f32[32]{0:T(128)S(1)} %get-tuple-element.60, f32[2,32,3,3,3]{1,4,0,3,2:T(4,128)S(1)} %copy-done.12), channel_id=1, replica_groups=mesh['gy'=8,'gz'=16] {'gy','gz'}, use_global_device_ids=true, to_apply=%region_4.5 | all-reduce | flops 3488 | bytes 27904 | tf_op jit(solution)/shard_map/psum | solution.py:199
  625.0 8.9 %reshape.857 = bf16[128,1,2,16,4,64]{5,4,3,2,1,0:T(4,128)(2,1)} reshape(bf16[128,2,4096]{2,1,0:T(2,128)(2,1)} %all-to-all-done.3) | data formatting | bytes 4194304
  633.9 10.7 %fusion.6 = bf16[2,16,4,64,128]{3,2,1,0,4:T(4,128)(2,1)} fusion(bf16[2,16,4,64,128]{3,2,1,0,4:T(4,128)(2,1)} %copy.230, bf16[2,16,4,64,128]{3,2,1,0,4:T(4,128)(2,1)} %copy.231, f32[4,64]{1,0:T(4,128)S(1)} %copy-done.15, bf16[128,1,2,16,4,64]{5,4,3,2,1,0:T(4,128)(2,1)} %reshape.857), kind=kLoop, calls=%fused_computation.11 | loop fusion | flops 8388608 | bytes 8389632 | tf_op jit(solution)/shard_map/convert_element_type | solution.py:177
  644.6 7.6 %copy.276 = bf16[2,16,4,64,128]{4,3,2,1,0:T(8,128)(2,1)} copy(bf16[2,16,4,64,128]{3,2,1,0,4:T(4,128)(2,1)} %fusion.6) | data formatting | bytes 4194304
  (204 shorter events, 120.2 us)
Async XLA Ops:
  14.1 19.7 %copy-start.4 = (bf16[2,16,4,64,128]{4,3,2,1,0:T(8,128)(2,1)S(1)}, bf16[2,16,4,64,128]{4,3,2,1,0:T(8,128)(2,1)}, u32[]{:S(2)}) copy-start(bf16[2,16,4,64,128]{4,3,2,1,0:T(8,128)(2,1)} %param.9) | copy-start | bytes 6291460
  21.9 46.7 %all-to-all-start = ((bf16[128,2,4096]{2,1,0:T(2,128)(2,1)}), bf16[128,2,4096]{2,1,0:T(2,128)(2,1)}, u32[]{:S(2)}, u32[]{:S(2)}) async-start(bf16[128,2,4096]{2,1,0:T(2,128)(2,1)} %reshape.850), calls=%async_computation | async-start | bytes 4194304 | tf_op jit(solution)/shard_map/all_to_all | solution.py:105
  33.9 5.4 copy-start.14
  33.9 6.0 copy-start.11
  54.0 8.4 %copy-start.10 = (bf16[2,16,4,64,128]{4,3,2,1,0:T(8,128)(2,1)S(1)}, bf16[2,16,4,64,128]{4,3,2,1,0:T(8,128)(2,1)}, u32[]{:S(2)}) copy-start(bf16[2,16,4,64,128]{4,3,2,1,0:T(8,128)(2,1)} %param.10) | copy-start | bytes 6291460
  68.5 52.0 %all-to-all-start.4 = ((bf16[128,2,4096]{2,1,0:T(2,128)(2,1)}), bf16[128,2,4096]{2,1,0:T(2,128)(2,1)S(1)}, u32[]{:S(2)}, u32[]{:S(2)}) async-start(bf16[128,2,4096]{2,1,0:T(2,128)(2,1)} %reshape.858), calls=%async_computation.4 | async-start | bytes 4194304 | tf_op jit(solution)/shard_map/all_to_all | solution.py:105
  86.4 7.6 %copy-start.6 = (bf16[128,1,2,4,16,64]{5,4,3,2,1,0:T(8,128)(2,1)S(1)}, bf16[128,1,2,4,16,64]{5,4,3,2,1,0:T(8,128)(2,1)}, u32[]{:S(2)}) copy-start(bf16[128,1,2,4,16,64]{5,4,3,2,1,0:T(8,128)(2,1)} %reshape.851) | copy-start | bytes 6291460
  114.8 3.0 copy-start.2
  117.8 12.5 %copy-start.17 = (s32[4,64]{1,0:T(4,128)S(1)}, s32[4,64]{1,0:T(4,128)}, u32[]{:S(2)}) copy-start(s32[4,64]{1,0:T(4,128)} %param.11) | copy-start | bytes 3076
  120.5 20.0 %all-to-all-start.1 = ((bf16[128,2,256]{2,1,0:T(2,128)(2,1)}), bf16[128,2,256]{2,1,0:T(2,128)(2,1)S(1)}, u32[]{:S(2)}, u32[]{:S(2)}) async-start(bf16[128,2,256]{2,1,0:T(2,128)(2,1)} %reshape.852), calls=%async_computation.1 | async-start | bytes 262144 | tf_op jit(solution)/shard_map/all_to_all | solution.py:117
  141.1 13.1 %collective-permute-start = (bf16[2,4,1,128]{2,1,0,3:T(4,128)(2,1)S(1)}, bf16[2,4,1,128]{2,1,0,3:T(4,128)(2,1)S(1)}, u32[]{:S(2)}, u32[]{:S(2)}) collective-permute-start(bf16[2,4,1,128]{2,1,0,3:T(4,128)(2,1)S(1)} %get-tuple-element.58), channel_id=1, source_target_pairs={{0,16},{16,32},{32,48},{48,64},{64,80},{80,96},{96,112},{1,17},{17... | collective-permute-start | bytes 6152 | tf_op jit(solution)/shard_map/ppermute | solution.py:17
  143.3 10.9 %collective-permute-start.1 = (bf16[2,4,1,128]{2,1,0,3:T(4,128)(2,1)S(1)}, bf16[2,4,1,128]{2,1,0,3:T(4,128)(2,1)S(1)}, u32[]{:S(2)}, u32[]{:S(2)}) collective-permute-start(bf16[2,4,1,128]{2,1,0,3:T(4,128)(2,1)S(1)} %get-tuple-element.59), channel_id=1, source_target_pairs={{16,0},{32,16},{48,32},{64,48},{80,64},{96,80},{112,96},{17,1},{33... | collective-permute-start | bytes 6152 | tf_op jit(solution)/shard_map/ppermute | solution.py:19
  144.6 15.8 %copy-start.5 = (bf16[128,1,2,4,16,64]{5,4,3,2,1,0:T(8,128)(2,1)S(1)}, bf16[128,1,2,4,16,64]{5,4,3,2,1,0:T(8,128)(2,1)}, u32[]{:S(2)}) copy-start(bf16[128,1,2,4,16,64]{5,4,3,2,1,0:T(8,128)(2,1)} %reshape.859) | copy-start | bytes 6291460
  155.0 12.7 %collective-permute-start.2 = (bf16[2,1,66,128]{2,1,0,3:T(2,128)(2,1)S(1)}, bf16[2,1,66,128]{2,1,0,3:T(2,128)(2,1)S(1)}, u32[]{:S(2)}, u32[]{:S(2)}) collective-permute-start(bf16[2,1,66,128]{2,1,0,3:T(2,128)(2,1)S(1)} %get-tuple-element.56), channel_id=1, source_target_pairs={{0,1},{1,2},{2,3},{3,4},{4,5},{5,6},{6,7},{7,8},{8,9},{9,10},{10,1... | collective-permute-start | bytes 101384 | tf_op jit(solution)/shard_map/ppermute | solution.py:17
  158.1 9.6 %collective-permute-start.3 = (bf16[2,1,66,128]{2,1,0,3:T(2,128)(2,1)S(1)}, bf16[2,1,66,128]{2,1,0,3:T(2,128)(2,1)S(1)}, u32[]{:S(2)}, u32[]{:S(2)}) collective-permute-start(bf16[2,1,66,128]{2,1,0,3:T(2,128)(2,1)S(1)} %get-tuple-element.57), channel_id=1, source_target_pairs={{1,0},{2,1},{3,2},{4,3},{5,4},{6,5},{7,6},{8,7},{9,8},{10,9},{11,1... | collective-permute-start | bytes 101384 | tf_op jit(solution)/shard_map/ppermute | solution.py:19
  205.4 3.5 copy-start.16
  211.8 2.1 copy-start
  211.8 6.8 %copy-start.7 = (f32[2,16,16,4,512]{4,2,3,1,0:T(8,128)S(1)}, f32[2,16,16,4,512]{4,2,3,1,0:T(8,128)}, u32[]{:S(2)}) copy-start(f32[2,16,16,4,512]{4,2,3,1,0:T(8,128)} %fusion.30) | copy-start | bytes 12582916
  211.8 6.8 %copy-start.8 = (f32[2,16,16,4,512]{4,2,3,1,0:T(8,128)S(1)}, f32[2,16,16,4,512]{4,2,3,1,0:T(8,128)}, u32[]{:S(2)}) copy-start(f32[2,16,16,4,512]{4,2,3,1,0:T(8,128)} %fusion.33) | copy-start | bytes 12582916
  214.0 7.2 %collective-permute-start.4 = (bf16[32,4,1,128]{3,0,2,1:T(8,128)(2,1)S(1)}, bf16[32,4,1,128]{3,0,2,1:T(8,128)(2,1)S(1)}, u32[]{:S(2)}, u32[]{:S(2)}) collective-permute-start(bf16[32,4,1,128]{3,0,2,1:T(8,128)(2,1)S(1)} %copy.347), channel_id=1, source_target_pairs={{0,16},{16,32},{32,48},{48,64},{64,80},{80,96},{96,112},{1,17},{17... | collective-permute-start | bytes 98312 | tf_op jit(solution)/shard_map/ppermute | solution.py:17
  219.9 4.7 collective-permute-start.5
  224.7 13.7 %collective-permute-start.6 = (bf16[32,1,66,128]{3,0,2,1:T(8,128)(2,1)S(1)}, bf16[32,1,66,128]{3,0,2,1:T(8,128)(2,1)S(1)}, u32[]{:S(2)}, u32[]{:S(2)}) collective-permute-start(bf16[32,1,66,128]{3,0,2,1:T(8,128)(2,1)S(1)} %get-tuple-element.41), channel_id=1, source_target_pairs={{0,1},{1,2},{2,3},{3,4},{4,5},{5,6},{6,7},{7,8},{8,9},{9,10},{10,1... | collective-permute-start | bytes 1622024 | tf_op jit(solution)/shard_map/ppermute | solution.py:17
  229.8 10.7 %collective-permute-start.7 = (bf16[32,1,66,128]{3,0,2,1:T(8,128)(2,1)S(1)}, bf16[32,1,66,128]{3,0,2,1:T(8,128)(2,1)S(1)}, u32[]{:S(2)}, u32[]{:S(2)}) collective-permute-start(bf16[32,1,66,128]{3,0,2,1:T(8,128)(2,1)S(1)} %get-tuple-element.42), channel_id=1, source_target_pairs={{1,0},{2,1},{3,2},{4,3},{5,4},{6,5},{7,6},{8,7},{9,8},{10,9},{11,1... | collective-permute-start | bytes 1622024 | tf_op jit(solution)/shard_map/ppermute | solution.py:19
  232.2 1.3 copy-start.1
  294.9 37.2 %all-to-all-start.2 = ((bf16[128,2,256]{2,1,0:T(2,128)(2,1)}), bf16[128,2,256]{2,1,0:T(2,128)(2,1)}, u32[]{:S(2)}, u32[]{:S(2)}) async-start(bf16[128,2,256]{2,1,0:T(2,128)(2,1)} %reshape.854), calls=%async_computation.2 | async-start | bytes 262144 | tf_op jit(solution)/shard_map/all_to_all | solution.py:153
  332.1 1.8 copy-start.3
  362.8 33.4 %all-to-all-start.5 = ((bf16[128,2,256]{2,1,0:T(2,128)(2,1)}), bf16[128,2,256]{2,1,0:T(2,128)(2,1)S(1)}, u32[]{:S(2)}, u32[]{:S(2)}) async-start(bf16[128,2,256]{2,1,0:T(2,128)(2,1)} %reshape.860), calls=%async_computation.5 | async-start | bytes 262144 | tf_op jit(solution)/shard_map/all_to_all | solution.py:117
  396.3 228.7 %all-to-all-start.3 = ((bf16[128,2,4096]{2,1,0:T(2,128)(2,1)}), bf16[128,2,4096]{2,1,0:T(2,128)(2,1)}, u32[]{:S(2)}, u32[]{:S(2)}) async-start(bf16[128,2,4096]{2,1,0:T(2,128)(2,1)} %reshape.856), calls=%async_computation.3 | async-start | bytes 4194304 | tf_op jit(solution)/shard_map/all_to_all | solution.py:169
  435.2 52.4 %collective-permute-start.8 = (bf16[2,4,1,128]{2,1,0,3:T(4,128)(2,1)S(1)}, bf16[2,4,1,128]{2,1,0,3:T(4,128)(2,1)S(1)}, u32[]{:S(2)}, u32[]{:S(2)}) collective-permute-start(bf16[2,4,1,128]{2,1,0,3:T(4,128)(2,1)S(1)} %get-tuple-element.52), channel_id=1, source_target_pairs={{0,16},{16,32},{32,48},{48,64},{64,80},{80,96},{96,112},{1,17},{17... | collective-permute-start | bytes 6152 | tf_op jit(solution)/shard_map/ppermute | solution.py:17
  438.5 49.1 %collective-permute-start.9 = (bf16[2,4,1,128]{2,1,0,3:T(4,128)(2,1)S(1)}, bf16[2,4,1,128]{2,1,0,3:T(4,128)(2,1)S(1)}, u32[]{:S(2)}, u32[]{:S(2)}) collective-permute-start(bf16[2,4,1,128]{2,1,0,3:T(4,128)(2,1)S(1)} %get-tuple-element.53), channel_id=1, source_target_pairs={{16,0},{32,16},{48,32},{64,48},{80,64},{96,80},{112,96},{17,1},{33... | collective-permute-start | bytes 6152 | tf_op jit(solution)/shard_map/ppermute | solution.py:19
  488.4 14.1 %collective-permute-start.10 = (bf16[2,1,66,128]{2,1,0,3:T(2,128)(2,1)S(1)}, bf16[2,1,66,128]{2,1,0,3:T(2,128)(2,1)S(1)}, u32[]{:S(2)}, u32[]{:S(2)}) collective-permute-start(bf16[2,1,66,128]{2,1,0,3:T(2,128)(2,1)S(1)} %get-tuple-element.50), channel_id=1, source_target_pairs={{0,1},{1,2},{2,3},{3,4},{4,5},{5,6},{6,7},{7,8},{8,9},{9,10},{10,1... | collective-permute-start | bytes 101384 | tf_op jit(solution)/shard_map/ppermute | solution.py:17
  492.2 10.3 %collective-permute-start.11 = (bf16[2,1,66,128]{2,1,0,3:T(2,128)(2,1)S(1)}, bf16[2,1,66,128]{2,1,0,3:T(2,128)(2,1)S(1)}, u32[]{:S(2)}, u32[]{:S(2)}) collective-permute-start(bf16[2,1,66,128]{2,1,0,3:T(2,128)(2,1)S(1)} %get-tuple-element.51), channel_id=1, source_target_pairs={{1,0},{2,1},{3,2},{4,3},{5,4},{6,5},{7,6},{8,7},{9,8},{10,9},{11,1... | collective-permute-start | bytes 101384 | tf_op jit(solution)/shard_map/ppermute | solution.py:19
  540.3 3.5 copy-start.13
  543.8 5.7 copy-start.9
  549.5 2.6 copy-start.12
  552.1 81.8 %copy-start.15 = (f32[4,64]{1,0:T(4,128)S(1)}, f32[4,64]{1,0:T(4,128)}, u32[]{:S(2)}) copy-start(f32[4,64]{1,0:T(4,128)} %convert_multiply_fusion.9) | copy-start | bytes 3076
where the time goes:
time: 664 us; the launch traced here: 653 us
  local copies, waits for them, and re-layouts  306 us (46%)
  starting transfers between devices  103 us (16%)
  matrix products  95.1 us (14%)
  blocking collectives  71.1 us (11%)
  other arithmetic  65.2 us (10%)
  waiting for transfers between devices  9.47 us (1%)
    unnamed x137, local copies, waits for them, and re-layouts  174 us
    psum x1, blocking collectives, on_device(): totals = lax.psum((grad_in, grad_bias, grad_out), ('gy', 'gz'))  71.1 us
    another operation x6, local copies, waits for them, and re-layouts, columns(): stacked = jnp.stack(pieces)  41.7 us
    dot_general x6, matrix products, transform(): jnp.einsum(formula, spectrum, tables[0], preferred_element_type=jnp.float32)  37.2 us
    dot_general x6, matrix products, transform(): jnp.einsum(formula, spectrum, tables[1], preferred_element_type=jnp.float32)  30.9 us
    dot_general x1, local copies, waits for them, and re-layouts, on_device(): jnp.einsum('fn,kn->fk', hidden_pad.reshape(channels, -1), grad_cols_wide,...  28 us
    ppermute x6, starting transfers between devices, with_halo(): lax.ppermute(tail, axis, [(i, (i + 1) % count) for i in range(ends)])  21.9 us
    all_to_all x2, starting transfers between devices, to_slices(): lax.all_to_all(stacked, ('gy', 'gz'), split_axis=1, concat_axis=1, tiled=...  21.7 us
  transfers between devices with their start and end apart: 18, of which 3 were waited for; matrix products, arithmetic and copies ran while one was open for 43% of the time, Pallas kernels for 0%

commit v1 on v0

v1 whole, which is shorter than its diff:
```python
import math

import jax
import jax.numpy as jnp
import numpy as np
from jax import lax
from jax.experimental import pallas as pl
from jax.experimental.pallas import tpu as pltpu
from jax.sharding import PartitionSpec as P

MESH = pl.DeviceIdType.MESH
AXES = ("gy", "gz")
BF = jnp.bfloat16
F32 = jnp.float32
VMEM_LIMIT = 56 * 2**20
VM = pl.BlockSpec(memory_space=pltpu.VMEM)


def trig(length):
    index = np.arange(length, dtype=np.int64)
    angle = (index[:, None] * index[None, :] % length).astype(np.float64) * (2.0 * math.pi / length)
    factor = 1.0 / math.sqrt(length)
    return np.cos(angle) * factor, np.sin(angle) * factor


def as_bf16(array):
    return np.asarray(array, dtype=np.float32).astype(jnp.bfloat16)


def inverse_y_table(gy, rows):
    length = gy * rows
    cos, sin = trig(length)
    cos, sin = cos.reshape(gy, rows, length), sin.reshape(gy, rows, length)
    table = np.stack([np.stack([cos, sin], 2), np.stack([-sin, cos], 2)], 1)
    return as_bf16(table.reshape(2 * length, 2 * length))


def forward_y_table(gy, rows):
    length = gy * rows
    cos, sin = trig(length)
    cos, sin = cos.reshape(length, gy, rows), sin.reshape(length, gy, rows)
    table = np.stack([np.stack([cos, -sin], 2), np.stack([sin, cos], 2)], 0)
    return as_bf16(table.reshape(2 * length, 2 * length))


def z_table(length, inverse):
    cos, sin = trig(length)
    if inverse:
        table = np.block([[cos, -sin], [sin, cos]])
    else:
        table = np.block([[cos, sin], [-sin, cos]])
    return as_bf16(table)


def band_masks():
    zo, dz, j, zi = np.ogrid[0:8, 0:3, 0:3, 0:8]
    return (8 * (j - 1) + zi == zo + dz - 1).astype(np.float32)


def band_spread():
    hit = band_masks()
    eye = np.eye(18, dtype=np.float32)
    spread = np.einsum("odjz,kl->odkjlz", hit, eye)
    return as_bf16(spread.reshape(8, 54, 432))


def band_keep():
    hit = band_masks()
    keep = np.broadcast_to(hit.transpose(1, 0, 2, 3)[:, :, :, None, :], (3, 8, 3, 18, 8))
    return np.ascontiguousarray(keep.reshape(3, 8, 432)).astype(np.float32)


def band_gather():
    eye = np.eye(18, dtype=np.float32)
    return np.ascontiguousarray(np.broadcast_to(eye[None, :, None, :], (3, 18, 8, 18)).reshape(432, 18))


def out_spread():
    q, dz, zo = np.ogrid[0:10, 0:3, 0:8]
    hit = (q == zo + dz).astype(np.float32)
    eye = np.eye(18, dtype=np.float32)
    return as_bf16(np.einsum("qdz,kl->qdklz", hit, eye).reshape(10, 54, 144))


def call(body, outs, scratch, name):
    return pl.pallas_call(
        body,
        out_shape=outs,
        scratch_shapes=scratch,
        compiler_params=pltpu.CompilerParams(vmem_limit_bytes=VMEM_LIMIT),
        name=name,
    )


def pack_body(k_ref, out_ref, stage):
    def block(index, carry):
        depth, coil = index // 16, index % 16
        both = jnp.concatenate([k_ref[0, coil, depth], k_ref[1, coil, depth]], axis=0)
        stage[pl.ds(index, 128, stride=64), :] = both.astype(F32).T
        return carry

    lax.fori_loop(0, 64, block, 0, unroll=2)

    def row(x, carry):
        out_ref[x] = stage[pl.ds(pl.multiple_of(x * 64, 64), 64), :].astype(BF)
        return carry

    lax.fori_loop(0, 128, row, 0, unroll=4)


def pack(kspace):
    return call(
        pack_body,
        jax.ShapeDtypeStruct((128, 64, 128), BF),
        [pltpu.VMEM((8192, 128), F32)],
        "pack",
    )(kspace)


def image_body(tiles, sens, table_y, table_z, out_ref, half):
    def rows(m, carry):
        left = jnp.concatenate(
            [tiles[pl.ds(gy * 16 + m * 4, 4)].reshape(256, 128) for gy in range(8)], axis=1
        )
        done = jnp.dot(left, table_y[...], preferred_element_type=F32)
        for lt in range(8):
            span = pl.ds(pl.multiple_of(lt * 1024 + m * 256, 256), 256)
            half[span, :] = done[:, lt * 128 : lt * 128 + 128]
        return carry

    lax.fori_loop(0, 4, rows, 0)

    def coil(c, carry):
        real, imag = carry
        lines = [half[pl.ds(lt * 1024 + c, 64, stride=16), :].astype(BF) for lt in range(8)]
        lines = [jnp.concatenate(lines[4 * p : 4 * p + 4], axis=1) for p in range(2)]
        lines = jnp.concatenate(lines, axis=0)
        coil_image = jnp.dot(table_z[...], lines, preferred_element_type=F32)
        c_r, c_i = coil_image[:64], coil_image[64:]
        s_r, s_i = sens[0, 0, c].astype(F32), sens[1, 0, c].astype(F32)
        return real + (s_r * c_r + s_i * c_i), imag + (s_r * c_i - s_i * c_r)

    zero = jnp.zeros((64, 512), F32)
    real, imag = lax.fori_loop(0, 16, coil, (zero, zero))
    out_ref[0] = real.astype(BF)
    out_ref[1] = imag.astype(BF)


def to_image(tiles, sens, table_y, table_z, name):
    return call(
        image_body,
        jax.ShapeDtypeStruct((2, 64, 512), BF),
        [pltpu.VMEM((8192, 128), F32)],
        name,
    )(tiles, sens, table_y, table_z)


def shifted(value, dy):
    if dy == 1:
        return value
    lane = lax.broadcasted_iota(jnp.int32, value.shape, value.ndim - 1)
    if dy == 0:
        return jnp.where(lane == 0, 0.0, pltpu.roll(value, 1, value.ndim - 1))
    return jnp.where(lane == 511, 0.0, pltpu.roll(value, 511, value.ndim - 1))


def fill_columns(images, cols):
    cols[pl.ds(0, 144), :] = jnp.zeros((144, 512), BF)
    cols[pl.ds(1296, 144), :] = jnp.zeros((144, 512), BF)
    for dx, image in enumerate(images):
        parts = [image[i].astype(F32) for i in range(2)]
        for dy in range(3):
            pair = jnp.stack([shifted(part, dy).reshape(8, 8, 512) for part in parts], axis=1)
            pair = pair.reshape(8, 16, 512).astype(BF)
            for zb in range(8):
                cols[pl.ds((zb + 1) * 144 + (dy * 3 + dx) * 16, 16), :] = pair[zb]


def forward_body(
    left, mid, right, w_in, bias, w_out, cols, hidden, slope, q_up, q_mid, q_down
):
    fill_columns((left, mid, right), cols)
    hidden[pl.ds(0, 32), :] = jnp.zeros((32, 512), BF)
    hidden[pl.ds(65 * 32, 32), :] = jnp.zeros((32, 512), BF)

    def block(zb, carry):
        window = cols[pl.ds(pl.multiple_of(zb * 144, 16), 432), :]
        pre = jnp.dot(w_in[...], window, preferred_element_type=F32) + bias[...]
        sig = jax.nn.sigmoid(pre)
        hidden[pl.ds(pl.multiple_of(zb * 256 + 32, 32), 256), :] = (pre * sig).astype(BF)
        slope[pl.ds(pl.multiple_of(zb * 256, 256), 256), :] = sig * (1.0 + pre * (1.0 - sig))
        return carry

    lax.fori_loop(0, 8, block, 0)

    def out(zb, carry):
        window = hidden[pl.ds(pl.multiple_of(zb * 256, 256), 320), :]
        terms = jnp.dot(w_out[...], window, preferred_element_type=F32).reshape(18, 8, 512)
        rows = pl.ds(pl.multiple_of(zb * 8, 8), 8)
        for dx, target in enumerate((q_up, q_mid, q_down)):
            for o in range(2):
                base = (dx * 2 + o) * 3
                total = shifted(terms[base], 0) + terms[base + 1] + shifted(terms[base + 2], 2)
                target[o, rows, :] = total
        return carry

    lax.fori_loop(0, 8, out, 0)


def conv_forward(left, mid, right, w_in, bias, w_out):
    part = jax.ShapeDtypeStruct((2, 64, 512), F32)
    return call(
        forward_body,
        (
            jax.ShapeDtypeStruct((1440, 512), BF),
            jax.ShapeDtypeStruct((66 * 32, 512), BF),
            jax.ShapeDtypeStruct((2048, 512), F32),
            part,
            part,
            part,
        ),
        [],
        "conv_forward",
    )(left, mid, right, w_in, bias, w_out)


def spread_body(q_from_left, q_mid, q_from_right, sens, table_z, table_y, out_ref, half):
    image = [
        (q_from_left[o].astype(F32) + q_mid[o] + q_from_right[o].astype(F32)).astype(BF).astype(F32)
        for o in range(2)
    ]
    r_r, r_i = image

    def coil(c, carry):
        s_r, s_i = sens[0, 0, c].astype(F32), sens[1, 0, c].astype(F32)
        lines = jnp.concatenate([s_r * r_r - s_i * r_i, s_r * r_i + s_i * r_r], axis=0).astype(BF)
        done = jnp.dot(table_z[...], lines, preferred_element_type=F32)
        for lt in range(8):
            p, lane = lt // 4, lt % 4 * 128
            half[pl.ds(lt * 1024 + c, 64, stride=16), :] = done[p * 64 : p * 64 + 64, lane : lane + 128]
        return carry

    lax.fori_loop(0, 16, coil, 0)

    def rows(m, carry):
        left = [half[pl.ds(pl.multiple_of(lt * 1024 + m * 256, 256), 256), :] for lt in range(8)]
        left = jnp.concatenate([part.astype(BF) for part in left], axis=1)
        done = jnp.dot(left, table_y[...], preferred_element_type=F32).astype(BF)
        for gy in range(8):
            out_ref[pl.ds(gy * 16 + m * 4, 4)] = done[:, gy * 128 : gy * 128 + 128].reshape(4, 64, 128)
        return carry

    lax.fori_loop(0, 4, rows, 0)


def to_coils(q_from_left, q_mid, q_from_right, sens, table_z, table_y):
    return call(
        spread_body,
        jax.ShapeDtypeStruct((128, 64, 128), BF),
        [pltpu.VMEM((8192, 128), F32)],
        "to_coils",
    )(q_from_left, q_mid, q_from_right, sens, table_z, table_y)


def unpack_body(tiles, kspace, measured, weight, out_ref, stage):
    def row(x, carry):
        stage[pl.ds(pl.multiple_of(x * 64, 64), 64), :] = tiles[x].astype(F32)
        return carry

    lax.fori_loop(0, 128, row, 0, unroll=4)

    def block(index, carry):
        depth, coil = index // 16, index % 16
        both = stage[pl.ds(index, 128, stride=64), :].T
        share = weight[depth]
        for part in range(2):
            current = kspace[part, coil, depth].astype(F32)
            other = measured[part, coil, depth].astype(F32)
            refine = both[part * 64 : part * 64 + 64]
            out_ref[part, coil, depth] = (current - share * (current - other) + refine).astype(BF)
        return carry

    lax.fori_loop(0, 64, block, 0, unroll=2)


def unpack(tiles, kspace, measured, weight):
    return call(
        unpack_body,
        jax.ShapeDtypeStruct((2, 16, 4, 64, 128), BF),
        [pltpu.VMEM((8192, 128), F32)],
        "unpack",
    )(tiles, kspace, measured, weight)


def gather_terms(total, keep, gather):
    pieces = []
    total = total.reshape(8, 32, 432)
    for dz in range(3):
        kept = total[0] * keep[dz, 0:1, :]
        for zo in range(1, 8):
            kept = kept + total[zo] * keep[dz, zo : zo + 1, :]
        pieces.append(
            jnp.dot(kept, gather[...], preferred_element_type=F32, precision=lax.Precision.HIGHEST)
        )
    return pieces


def backward_body(
    left, mid, right, cols, hidden, slope, w_back, keep, gather, out_ref, cols_g, sum_in, sum_out, sum_b
):
    fill_columns((left, mid, right), cols_g)
    sum_in[...] = jnp.zeros_like(sum_in)
    sum_out[...] = jnp.zeros_like(sum_out)
    sum_b[...] = jnp.zeros_like(sum_b)
    nt = (((1,), (1,)), ((), ()))

    def block(zb, carry):
        span = pl.ds(pl.multiple_of(zb * 144, 16), 432)
        window_g = cols_g[span, :]
        back = jnp.dot(w_back[...], window_g, preferred_element_type=F32)
        back = (back * slope[pl.ds(pl.multiple_of(zb * 256, 256), 256), :]).astype(BF)
        sum_in[...] += lax.dot_general(back, cols[span, :], nt, preferred_element_type=F32)
        held = hidden[pl.ds(pl.multiple_of(zb * 256 + 32, 32), 256), :]
        sum_out[...] += lax.dot_general(held, window_g, nt, preferred_element_type=F32)
        wide = back.astype(F32)
        sum_b[...] += wide[:, :128] + wide[:, 128:256] + wide[:, 256:384] + wide[:, 384:]
        return carry

    lax.fori_loop(0, 8, block, 0)
    bias_sum = jnp.sum(sum_b[...].reshape(8, 32, 128), axis=0)
    bias_sum = jnp.sum(bias_sum, axis=1, keepdims=True)
    pieces = gather_terms(sum_in[...], keep, gather) + gather_terms(sum_out[...], keep, gather)
    pieces.append(jnp.broadcast_to(bias_sum, (32, 20)))
    out_ref[...] = jnp.concatenate(pieces, axis=1)


def conv_backward(left, mid, right, cols, hidden, slope, w_back, keep, gather):
    return call(
        backward_body,
        jax.ShapeDtypeStruct((32, 128), F32),
        [
            pltpu.VMEM((1440, 512), BF),
            pltpu.VMEM((256, 432), F32),
            pltpu.VMEM((256, 432), F32),
            pltpu.VMEM((256, 128), F32),
        ],
        "conv_backward",
    )(left, mid, right, cols, hidden, slope, w_back, keep, gather)


def reduce_body(count_y, count_z, in_ref, out_ref, first, second, sems):
    my_y, my_z = lax.axis_index("gy"), lax.axis_index("gz")

    def exchange(value, buffer, count, mine, device, send, recv):
        buffer[mine] = value

        def start(step, carry):
            to = lax.rem(mine + step, count)
            pltpu.make_async_remote_copy(
                src_ref=buffer.at[mine],
                dst_ref=buffer.at[mine],
                send_sem=send,
                recv_sem=recv,
                device_id=device(to),
                device_id_type=MESH,
            ).start()
            return carry

        lax.fori_loop(1, count, start, 0)
        every = pltpu.make_async_remote_copy(
            src_ref=buffer.at[pl.ds(0, count - 1)],
            dst_ref=buffer.at[pl.ds(0, count - 1)],
            send_sem=send,
            recv_sem=recv,
            device_id=device(mine),
            device_id_type=MESH,
        )
        every.wait_send()
        every.wait_recv()
        total = buffer[0]
        for index in range(1, count):
            total = total + buffer[index]
        return total

    over_z = exchange(
        in_ref[...], first, count_z, my_z, lambda to: (my_y, to), sems.at[0], sems.at[1]
    )
    out_ref[...] = exchange(
        over_z, second, count_y, my_y, lambda to: (to, my_z), sems.at[2], sems.at[3]
    )


def all_reduce(value, count_y, count_z):
    def body(*refs):
        reduce_body(count_y, count_z, *refs)

    return pl.pallas_call(
        body,
        out_shape=jax.ShapeDtypeStruct((32, 128), F32),
        in_specs=[VM],
        out_specs=VM,
        scratch_shapes=[
            pltpu.VMEM((count_z, 32, 128), F32),
            pltpu.VMEM((count_y, 32, 128), F32),
            pltpu.SemaphoreType.DMA((4,)),
        ],
        compiler_params=pltpu.CompilerParams(has_side_effects=True),
        name="all_reduce",
    )(value)


def on_device(
    kspace, measured, sample_mask, step_size, coil_field, conv_in, bias_in, conv_out, cotangent
):
    count_y, count_z = lax.axis_size("gy"), lax.axis_size("gz")
    devices = count_y * count_z
    row_tile, x_cells, depth_tile = kspace.shape[3], kspace.shape[4], kspace.shape[2]
    inverse_y = jnp.asarray(inverse_y_table(count_y, row_tile))
    forward_y = jnp.asarray(forward_y_table(count_y, row_tile))
    inverse_z = jnp.asarray(z_table(count_z * depth_tile, True))
    forward_z = jnp.asarray(z_table(count_z * depth_tile, False))
    spread = jnp.asarray(band_spread())
    keep = jnp.asarray(band_keep())
    gather = jnp.asarray(band_gather())
    spread_out = jnp.asarray(out_spread())

    flat_in = conv_in.transpose(0, 2, 3, 4, 1).reshape(32, 54)
    w_in = jnp.einsum("ok,zkc->zoc", flat_in, spread).reshape(256, 432)
    flat_back = conv_out[:, :, ::-1, ::-1, ::-1].transpose(1, 2, 3, 4, 0).reshape(32, 54)
    w_back = jnp.einsum("ok,zkc->zoc", flat_back, spread).reshape(256, 432)
    flat_out = conv_out.transpose(1, 2, 4, 0, 3).reshape(32, 54)
    w_out = jnp.einsum("ik,qkr->rqi", flat_out, spread_out).reshape(144, 320)
    bias = jnp.tile(bias_in, 8)[:, None]
    weight = jnp.broadcast_to(
        (step_size[0] * sample_mask.astype(F32))[:, :, None], (depth_tile, row_tile, x_cells)
    )

    def exchange(blocks):
        return lax.all_to_all(blocks, AXES, split_axis=0, concat_axis=0, tiled=True)

    up = [(i, i + 1) for i in range(devices - 1)]
    down = [(i + 1, i) for i in range(devices - 1)]

    def neighbours(image):
        return lax.ppermute(image, AXES, up), lax.ppermute(image, AXES, down)

    k_tiles = exchange(pack(kspace))
    g_tiles = exchange(pack(cotangent))
    image = to_image(k_tiles, coil_field, inverse_y, inverse_z, "image_k")
    left, right = neighbours(image)
    cols, hidden, slope, q_up, q_mid, q_down = conv_forward(left, image, right, w_in, bias, w_out)
    from_left = lax.ppermute(q_up, AXES, up)
    from_right = lax.ppermute(q_down, AXES, down)
    blocks = to_coils(from_left, q_mid, from_right, coil_field, forward_z, forward_y)
    refine = exchange(blocks)
    grad = to_image(g_tiles, coil_field, inverse_y, inverse_z, "image_g")
    g_left, g_right = neighbours(grad)
    terms = conv_backward(g_left, grad, g_right, cols, hidden, slope, w_back, keep, gather)
    totals = all_reduce(terms, count_y, count_z)
    kspace_next = unpack(refine, kspace, measured, weight)

    norm = 1.0 / math.sqrt(x_cells * row_tile * count_y * depth_tile * count_z)
    totals = totals * norm
    grad_in = totals[:, :54].reshape(32, 3, 3, 3, 2).transpose(0, 4, 1, 2, 3)
    grad_out = totals[:, 54:108].reshape(32, 3, 3, 3, 2).transpose(4, 0, 1, 2, 3)
    grad_out = grad_out[:, :, ::-1, ::-1, ::-1]
    return kspace_next, grad_in, totals[:, 108], grad_out


def solution(mesh):
    tile = P(None, None, "gz", "gy", None)
    in_specs = (
        tile,
        tile,
        P("gz", "gy"),
        P(),
        P(None, AXES, None, None, None),
        P(),
        P(),
        P(),
        tile,
    )
    out_specs = (tile, P(), P(), P())
    return jax.shard_map(
        on_device, mesh=mesh, in_specs=in_specs, out_specs=out_specs, check_vma=False
    )
```

time: 664 us -> 211 us (0.32); the launches traced: 653 us -> 211 us
  local copies, waits for them, and re-layouts: 306 us -> 9.48 us
  Pallas kernels: 0 us -> 106 us
  matrix products: 95.1 us -> 2.21 us
  blocking collectives: 71.1 us -> 0 us
  other arithmetic: 65.2 us -> 0.73 us
  starting transfers between devices: 103 us -> 48.1 us
  waiting for transfers between devices: 9.47 us -> 42.3 us
    unnamed x137 -> x31, local copies, waits for them, and re-layouts: 174 us -> 4.88 us
    pallas_call x0 -> x9, Pallas kernels: none -> 106 us  [the longest x2 23.4 us: to_image(): call(image_body, jax.ShapeDtypeStruct((2, 64, 512), BF), [pltpu.VMEM((819...]
    dot_general x17 -> x3, matrix products: 95.1 us -> 2.21 us  [the longest x1 0.99 us: on_device(): w_back = jnp.einsum('ok,zkc->zoc', flat_back, spread).reshape(256, 432)]
    psum x1 -> x0, blocking collectives: 71.1 us -> none  [on_device(): totals = lax.psum((grad_in, grad_bias, grad_out), ('gy', 'gz'))]
    reshape x11 -> x5, local copies, waits for them, and re-layouts: 49.7 us -> 1.45 us  [the longest x1 0.74 us: on_device(): w_out = jnp.einsum('ik,qkr->rqi', flat_out, spread_out).reshape(144, 320)]
    another operation x12 -> x2, local copies, waits for them, and re-layouts: 44.6 us -> 0.78 us  [on_device(): bias = jnp.tile(bias_in, 8)[:, None]]
    all_to_all x6 -> x3, starting transfers between devices: 70.9 us -> 30.8 us  [exchange(): return lax.all_to_all(blocks, AXES, split_axis=0, concat_axis=0, tiled=True)]
    dot_general x2 -> x1, local copies, waits for them, and re-layouts: 30.6 us -> 0.02 us  [on_device(): w_in = jnp.einsum('ok,zkc->zoc', flat_in, spread).reshape(256, 432)]
  transfers between devices with their start and end apart: 18 -> 9, of which waited for: 3 -> 5; matrix products, arithmetic and copies ran while one was open for 43% -> 3% of each run, Pallas kernels for 0% -> 42%
where the time goes in v1:
time: 211 us
  Pallas kernels  106 us (50%)
  starting transfers between devices  48.1 us (23%)
  waiting for transfers between devices  42.3 us (20%)
  local copies, waits for them, and re-layouts  9.48 us (4%)
  matrix products  2.21 us (1%)
    all_to_all x3, starting transfers between devices, exchange(): return lax.all_to_all(blocks, AXES, split_axis=0, concat_axis=0, tiled=True)  30.8 us
    pallas_call x2, Pallas kernels, to_image(): call(image_body, jax.ShapeDtypeStruct((2, 64, 512), BF), [pltpu.VMEM((819...  23.4 us
    pallas_call x1, Pallas kernels, all_reduce(): pl.pallas_call(body, out_shape=jax.ShapeDtypeStruct((32, 128), F32), in_s...  23.2 us
    all_to_all x3, waiting for transfers between devices, exchange(): return lax.all_to_all(blocks, AXES, split_axis=0, concat_axis=0, tiled=True)  21.9 us
    pallas_call x2, Pallas kernels, pack(): call(pack_body, jax.ShapeDtypeStruct((128, 64, 128), BF), [pltpu.VMEM((81...  17.5 us
    ppermute x4, waiting for transfers between devices, neighbours(): return (lax.ppermute(image, AXES, up), lax.ppermute(image, AXES, down))  14.5 us
    pallas_call x1, Pallas kernels, to_coils(): call(spread_body, jax.ShapeDtypeStruct((128, 64, 128), BF), [pltpu.VMEM((...  12 us
    ppermute x4, starting transfers between devices, neighbours(): return (lax.ppermute(image, AXES, up), lax.ppermute(image, AXES, down))  11.1 us
  transfers between devices with their start and end apart: 9, of which 5 were waited for; matrix products, arithmetic and copies ran while one was open for 3% of the time, Pallas kernels for 42%

profile of v1, /device:TPU:1, one launch (start us, length us, event | category | flops | bytes accessed | tf_op | source)
XLA Modules:
  0.0 210.5 jit_solution(4946821768720726661)
XLA Ops:
  0.6 8.7 %pack.2 = bf16[128,64,128]{2,1,0:T(8,128)(2,1)} custom-call(bf16[2,16,4,64,128]{4,3,2,1,0:T(8,128)(2,1)} %kspace.1), custom_call_target="tpu_custom_call" | custom-call | tf_op jit(solution)/shard_map/pack/pallas_call | solution.py:112
  9.3 11.5 %all-to-all-start = ((bf16[128,64,128]{2,1,0:T(8,128)(2,1)}), bf16[128,64,128]{2,1,0:T(8,128)(2,1)S(1)}, u32[]{:S(2)}, u32[]{:S(2)}) async-start(bf16[128,64,128]{2,1,0:T(8,128)(2,1)} %pack.2), calls=%async_computation | async-start | bytes 4194304 | tf_op jit(solution)/shard_map/all_to_all | solution.py:439
  20.8 8.8 %pack.3 = bf16[128,64,128]{2,1,0:T(8,128)(2,1)} custom-call(bf16[2,16,4,64,128]{4,3,2,1,0:T(8,128)(2,1)} %k_ref.3), custom_call_target="tpu_custom_call" | custom-call | tf_op jit(solution)/shard_map/pack/pallas_call | solution.py:112
  29.6 0.0 copy-start.12
  29.6 0.0 copy-start.11
  29.6 0.0 copy-start.14
  29.6 0.0 copy-start.4
  29.6 21.9 %all-to-all-done.tiles = bf16[128,64,128]{2,1,0:T(8,128)(2,1)S(1)} async-done(((bf16[128,64,128]{2,1,0:T(8,128)(2,1)}), bf16[128,64,128]{2,1,0:T(8,128)(2,1)S(1)}, u32[]{:S(2)}, u32[]{:S(2)}) %all-to-all-start) | async-done | bytes 2097184 | tf_op jit(solution)/shard_map/all_to_all | solution.py:439
  51.5 1.3 copy-done.1
  52.8 4.1 %all-to-all-start.2 = ((bf16[128,64,128]{2,1,0:T(8,128)(2,1)}), bf16[128,64,128]{2,1,0:T(8,128)(2,1)S(1)}, u32[]{:S(2)}, u32[]{:S(2)}) async-start(bf16[128,64,128]{2,1,0:T(8,128)(2,1)} %pack.3), calls=%async_computation.2 | async-start | bytes 4194304 | tf_op jit(solution)/shard_map/all_to_all | solution.py:439
  57.0 0.0 copy-done.12
  57.0 0.0 copy-done.11
  57.1 0.0 copy-done.14
  57.1 0.8 broadcast_in_dim_tile.4.bias
  57.9 0.0 copy-done.4
  57.9 0.2 fusion
  58.1 0.7 copy.30.w_out
  58.9 0.0 copy-start.3
  58.9 11.7 %image_k.1.mid = bf16[2,64,512]{2,1,0:T(8,128)(2,1)} custom-call(bf16[128,64,128]{2,1,0:T(8,128)(2,1)} %copy-done.1, bf16[2,1,16,64,512]{4,3,2,1,0:T(8,128)(2,1)} %sens.5, bf16[1024,1024]{1,0:T(8,128)(2,1)} %constant.18.clone.table_y, bf16[128,128]{1,0:T(8,128)(2,1)} %constant.20.clone.table_z), custom_call_target="tpu_custom_call" | custom-call | tf_op jit(solution)/shard_map/image_k/pallas_call | solution.py:150
  70.6 3.0 %collective-permute-start.1 = (bf16[2,64,512]{2,1,0:T(8,128)(2,1)}, bf16[2,64,512]{2,1,0:T(8,128)(2,1)S(1)}, u32[]{:S(2)}, u32[]{:S(2)}) collective-permute-start(bf16[2,64,512]{2,1,0:T(8,128)(2,1)} %image_k.1.mid), channel_id=1, source_target_pairs={{1,0},{2,1},{3,2},{4,3},{5,4},{6,5},{7,6},{8,7},{9,8},{10,9},{11,1... | collective-permute-start | bytes 393224 | tf_op jit(solution)/shard_map/ppermute | solution.py:445
  73.6 2.6 %collective-permute-start = (bf16[2,64,512]{2,1,0:T(8,128)(2,1)}, bf16[2,64,512]{2,1,0:T(8,128)(2,1)S(1)}, u32[]{:S(2)}, u32[]{:S(2)}) collective-permute-start(bf16[2,64,512]{2,1,0:T(8,128)(2,1)} %image_k.1.mid), channel_id=1, source_target_pairs={{0,1},{1,2},{2,3},{3,4},{4,5},{5,6},{6,7},{7,8},{8,9},{9,10},{10,1... | collective-permute-start | bytes 393224 | tf_op jit(solution)/shard_map/ppermute | solution.py:445
  76.2 0.0 copy-done.3
  76.2 1.0 fusion.4
  77.2 6.8 %collective-permute-done.1.right = bf16[2,64,512]{2,1,0:T(8,128)(2,1)S(1)} collective-permute-done((bf16[2,64,512]{2,1,0:T(8,128)(2,1)}, bf16[2,64,512]{2,1,0:T(8,128)(2,1)S(1)}, u32[]{:S(2)}, u32[]{:S(2)}) %collective-permute-start.1) | collective-permute-done | bytes 131104 | tf_op jit(solution)/shard_map/ppermute | solution.py:445
  84.0 0.0 copy-start.9
  84.0 0.0 collective-permute-done.left
  84.0 0.0 copy-start.10
  84.0 0.6 copy-done.9
  84.6 0.1 copy-done.10
  84.7 10.3 %conv_forward.1 = (bf16[1440,512]{1,0:T(8,128)(2,1)}, bf16[2112,512]{1,0:T(8,128)(2,1)}, f32[2048,512]{1,0:T(8,128)}, f32[2,64,512]{2,1,0:T(8,128)}, f32[2,64,512]{2,1,0:T(8,128)}, /*index=5*/f32[2,64,512]{2,1,0:T(8,128)}) custom-call(bf16[2,64,512]{2,1,0:T(8,128)(2,1)} %copy-done.10, bf16[2,64,512]{2,1,0:T(8,128)(2,1)} %image_k.1.mid, ...), custom_call_target="tpu_custom_call" | custom-call | tf_op jit(solution)/shard_map/conv_forward/pallas_call | solution.py:212
  95.0 4.2 %collective-permute-start.2 = (f32[2,64,512]{2,1,0:T(8,128)}, f32[2,64,512]{2,1,0:T(8,128)S(1)}, u32[]{:S(2)}, u32[]{:S(2)}) collective-permute-start(f32[2,64,512]{2,1,0:T(8,128)} %get-tuple-element.10), channel_id=1, source_target_pairs={{0,1},{1,2},{2,3},{3,4},{4,5},{5,6},{6,7},{7,8},{8,9},{9,10},{10,1... | collective-permute-start | bytes 786440 | tf_op jit(solution)/shard_map/ppermute | solution.py:452
  99.2 1.9 collective-permute-start.3
  101.2 1.7 collective-permute-done.2.q_from_left
  102.8 0.0 copy-start.5
  102.8 4.3 %collective-permute-done.3.q_from_right = f32[2,64,512]{2,1,0:T(8,128)S(1)} collective-permute-done((f32[2,64,512]{2,1,0:T(8,128)}, f32[2,64,512]{2,1,0:T(8,128)S(1)}, u32[]{:S(2)}, u32[]{:S(2)}) %collective-permute-start.3) | collective-permute-done | bytes 262176 | tf_op jit(solution)/shard_map/ppermute | solution.py:453
  107.1 0.0 copy-start.6
  107.1 0.0 copy-done.5
  107.1 0.7 copy-done.6
  107.9 12.0 %to_coils.1 = bf16[128,64,128]{2,1,0:T(8,128)(2,1)} custom-call(f32[2,64,512]{2,1,0:T(8,128)} %copy-done.5, f32[2,64,512]{2,1,0:T(8,128)} %get-tuple-element.11.q_mid, f32[2,64,512]{2,1,0:T(8,128)} %copy-done.6, bf16[2,1,16,64,512]{4,3,2,1,0:T(8,128)(2,1)} %sens.5, bf16[128,128]{1,0:T(8,128)(2,1)} %constant.21.clone.table_z, ...), custom_call_target="tpu_custom_call" | custom-call | tf_op jit(solution)/shard_map/to_coils/pallas_call | solution.py:257
  119.8 0.0 all-to-all-done.2.tiles
  119.8 1.4 copy-done
  121.2 15.2 %all-to-all-start.1 = ((bf16[128,64,128]{2,1,0:T(8,128)(2,1)}), bf16[128,64,128]{2,1,0:T(8,128)(2,1)}, u32[]{:S(2)}, u32[]{:S(2)}) async-start(bf16[128,64,128]{2,1,0:T(8,128)(2,1)} %to_coils.1), calls=%async_computation.1 | async-start | bytes 4194304 | tf_op jit(solution)/shard_map/all_to_all | solution.py:439
  137.1 0.0 copy-done.2
  137.1 1.0 fusion.2
  138.1 11.7 %image_g.1.mid = bf16[2,64,512]{2,1,0:T(8,128)(2,1)} custom-call(bf16[128,64,128]{2,1,0:T(8,128)(2,1)} %copy-done, bf16[2,1,16,64,512]{4,3,2,1,0:T(8,128)(2,1)} %sens.5, bf16[1024,1024]{1,0:T(8,128)(2,1)} %constant.18.clone.table_y, bf16[128,128]{1,0:T(8,128)(2,1)} %constant.20.clone.table_z), custom_call_target="tpu_custom_call" | custom-call | tf_op jit(solution)/shard_map/image_g/pallas_call | solution.py:150
  149.8 3.0 %collective-permute-start.5 = (bf16[2,64,512]{2,1,0:T(8,128)(2,1)}, bf16[2,64,512]{2,1,0:T(8,128)(2,1)S(1)}, u32[]{:S(2)}, u32[]{:S(2)}) collective-permute-start(bf16[2,64,512]{2,1,0:T(8,128)(2,1)} %image_g.1.mid), channel_id=1, source_target_pairs={{1,0},{2,1},{3,2},{4,3},{5,4},{6,5},{7,6},{8,7},{9,8},{10,9},{11,1... | collective-permute-start | bytes 393224 | tf_op jit(solution)/shard_map/ppermute | solution.py:445
  152.8 2.5 %collective-permute-start.4 = (bf16[2,64,512]{2,1,0:T(8,128)(2,1)}, bf16[2,64,512]{2,1,0:T(8,128)(2,1)S(1)}, u32[]{:S(2)}, u32[]{:S(2)}) collective-permute-start(bf16[2,64,512]{2,1,0:T(8,128)(2,1)} %image_g.1.mid), channel_id=1, source_target_pairs={{0,1},{1,2},{2,3},{3,4},{4,5},{5,6},{6,7},{7,8},{8,9},{9,10},{10,1... | collective-permute-start | bytes 393224 | tf_op jit(solution)/shard_map/ppermute | solution.py:445
  155.4 0.0 copy-done.13
  155.4 7.7 %collective-permute-done.5.right = bf16[2,64,512]{2,1,0:T(8,128)(2,1)S(1)} collective-permute-done((bf16[2,64,512]{2,1,0:T(8,128)(2,1)}, bf16[2,64,512]{2,1,0:T(8,128)(2,1)S(1)}, u32[]{:S(2)}, u32[]{:S(2)}) %collective-permute-start.5) | collective-permute-done | bytes 131104 | tf_op jit(solution)/shard_map/ppermute | solution.py:445
  163.1 0.0 collective-permute-done.4.left
  163.1 0.7 copy-done.7
  163.8 0.1 copy-done.8
  163.8 10.6 %conv_backward.1.refs_0_ = f32[32,128]{1,0:T(8,128)} custom-call(bf16[2,64,512]{2,1,0:T(8,128)(2,1)} %copy-done.8, bf16[2,64,512]{2,1,0:T(8,128)(2,1)} %image_g.1.mid, bf16[2,64,512]{2,1,0:T(8,128)(2,1)} %copy-done.7, bf16[1440,512]{1,0:T(8,128)(2,1)} %get-tuple-element.13.cols, bf16[2112,512]{1,0:T(8,128)(2,1)} %get-tuple-element.14.hidden, ...), custom_call_target="tpu_custom_call" | custom-call | tf_op jit(solution)/shard_map/conv_backward/pallas_call | solution.py:338
  174.4 23.2 %all_reduce.1 = f32[32,128]{1,0:T(8,128)} custom-call(f32[32,128]{1,0:T(8,128)} %conv_backward.1.refs_0_), custom_call_target="tpu_custom_call" | custom-call | tf_op jit(solution)/shard_map/all_reduce/pallas_call | solution.py:397
  197.6 0.7 broadcast_multiply_fusion
  198.3 0.1 fusion.6
  198.4 0.1 copy.33
  198.5 0.6 rev.7
  199.1 0.1 copy.32
  199.2 0.6 reshape.40
  199.9 0.7 slice_reduce_fusion
  200.6 0.0 all-to-all-done.1.tiles
  200.6 0.8 broadcast_in_dim.2.weight
  201.3 9.2 %unpack.1 = bf16[2,16,4,64,128]{4,3,2,1,0:T(8,128)(2,1)} custom-call(bf16[128,64,128]{2,1,0:T(8,128)(2,1)} %all-to-all-done.1.tiles, bf16[2,16,4,64,128]{4,3,2,1,0:T(8,128)(2,1)} %kspace.1, bf16[2,16,4,64,128]{4,3,2,1,0:T(8,128)(2,1)} %measured.1, f32[4,64,128]{2,1,0:T(8,128)} %broadcast_in_dim.2.weight), custom_call_target="tpu_custom_call" | custom-call | tf_op jit(solution)/shard_map/unpack/pallas_call | solution.py:287
  (15 shorter events, 0.1 us)
Async XLA Ops:
  9.3 42.2 %all-to-all-start = ((bf16[128,64,128]{2,1,0:T(8,128)(2,1)}), bf16[128,64,128]{2,1,0:T(8,128)(2,1)S(1)}, u32[]{:S(2)}, u32[]{:S(2)}) async-start(bf16[128,64,128]{2,1,0:T(8,128)(2,1)} %pack.2), calls=%async_computation | async-start | bytes 4194304 | tf_op jit(solution)/shard_map/all_to_all | solution.py:439
  29.6 27.4 %copy-start.12 = (bf16[32,2,3,3,3]{0,1,4,3,2:T(2,128)(2,1)S(1)}, bf16[32,2,3,3,3]{0,1,4,3,2:T(2,128)(2,1)}, u32[]{:S(2)}) copy-start(bf16[32,2,3,3,3]{0,1,4,3,2:T(2,128)(2,1)} %param.22) | copy-start | bytes 10372
  29.6 27.4 %copy-start.11 = (bf16[2,32,3,3,3]{1,0,4,3,2:T(2,128)(2,1)S(1)}, bf16[2,32,3,3,3]{1,0,4,3,2:T(2,128)(2,1)}, u32[]{:S(2)}) copy-start(bf16[2,32,3,3,3]{1,0,4,3,2:T(2,128)(2,1)} %param.24) | copy-start | bytes 10372
  29.6 27.5 %copy-start.14 = (f32[32]{0:T(128)S(1)}, f32[32]{0:T(128)}, u32[]{:S(2)}) copy-start(f32[32]{0:T(128)} %param.23) | copy-start | bytes 388
  29.6 28.3 %copy-start.4 = (bf16[10,54,144]{2,1,0:T(8,128)(2,1)S(1)}, bf16[10,54,144]{2,1,0:T(8,128)(2,1)}, u32[]{:S(2)}) copy-start(bf16[10,54,144]{2,1,0:T(8,128)(2,1)} %constant.25.clone) | copy-start | bytes 466564
  51.5 1.3 copy-start.1
  52.8 67.0 %all-to-all-start.2 = ((bf16[128,64,128]{2,1,0:T(8,128)(2,1)}), bf16[128,64,128]{2,1,0:T(8,128)(2,1)S(1)}, u32[]{:S(2)}, u32[]{:S(2)}) async-start(bf16[128,64,128]{2,1,0:T(8,128)(2,1)} %pack.3), calls=%async_computation.2 | async-start | bytes 4194304 | tf_op jit(solution)/shard_map/all_to_all | solution.py:439
  58.9 17.3 %copy-start.3 = (bf16[8,54,432]{2,1,0:T(8,128)(2,1)S(1)}, bf16[8,54,432]{2,1,0:T(8,128)(2,1)}, u32[]{:S(2)}) copy-start(bf16[8,54,432]{2,1,0:T(8,128)(2,1)} %constant.33) | copy-start | bytes 1119748
  70.6 13.4 %collective-permute-start.1 = (bf16[2,64,512]{2,1,0:T(8,128)(2,1)}, bf16[2,64,512]{2,1,0:T(8,128)(2,1)S(1)}, u32[]{:S(2)}, u32[]{:S(2)}) collective-permute-start(bf16[2,64,512]{2,1,0:T(8,128)(2,1)} %image_k.1.mid), channel_id=1, source_target_pairs={{1,0},{2,1},{3,2},{4,3},{5,4},{6,5},{7,6},{8,7},{9,8},{10,9},{11,1... | collective-permute-start | bytes 393224 | tf_op jit(solution)/shard_map/ppermute | solution.py:445
  73.6 10.4 %collective-permute-start = (bf16[2,64,512]{2,1,0:T(8,128)(2,1)}, bf16[2,64,512]{2,1,0:T(8,128)(2,1)S(1)}, u32[]{:S(2)}, u32[]{:S(2)}) collective-permute-start(bf16[2,64,512]{2,1,0:T(8,128)(2,1)} %image_k.1.mid), channel_id=1, source_target_pairs={{0,1},{1,2},{2,3},{3,4},{4,5},{5,6},{6,7},{7,8},{8,9},{9,10},{10,1... | collective-permute-start | bytes 393224 | tf_op jit(solution)/shard_map/ppermute | solution.py:445
  84.0 0.7 copy-start.9
  84.0 0.7 copy-start.10
  95.0 7.8 %collective-permute-start.2 = (f32[2,64,512]{2,1,0:T(8,128)}, f32[2,64,512]{2,1,0:T(8,128)S(1)}, u32[]{:S(2)}, u32[]{:S(2)}) collective-permute-start(f32[2,64,512]{2,1,0:T(8,128)} %get-tuple-element.10), channel_id=1, source_target_pairs={{0,1},{1,2},{2,3},{3,4},{4,5},{5,6},{6,7},{7,8},{8,9},{9,10},{10,1... | collective-permute-start | bytes 786440 | tf_op jit(solution)/shard_map/ppermute | solution.py:452
  99.2 7.9 %collective-permute-start.3 = (f32[2,64,512]{2,1,0:T(8,128)}, f32[2,64,512]{2,1,0:T(8,128)S(1)}, u32[]{:S(2)}, u32[]{:S(2)}) collective-permute-start(f32[2,64,512]{2,1,0:T(8,128)} %get-tuple-element.12), channel_id=1, source_target_pairs={{1,0},{2,1},{3,2},{4,3},{5,4},{6,5},{7,6},{8,7},{9,8},{10,9},{11,1... | collective-permute-start | bytes 786440 | tf_op jit(solution)/shard_map/ppermute | solution.py:453
  102.8 4.3 %copy-start.5 = (f32[2,64,512]{2,1,0:T(8,128)}, f32[2,64,512]{2,1,0:T(8,128)S(1)}, u32[]{:S(2)}) copy-start(f32[2,64,512]{2,1,0:T(8,128)S(1)} %collective-permute-done.2.q_from_left) | copy-start | bytes 786436
  107.1 0.7 copy-start.6
  119.8 17.3 %copy-start.2 = (bf16[8,54,432]{2,1,0:T(8,128)(2,1)S(1)}, bf16[8,54,432]{2,1,0:T(8,128)(2,1)}, u32[]{:S(2)}) copy-start(bf16[8,54,432]{2,1,0:T(8,128)(2,1)} %constant.22.clone) | copy-start | bytes 1119748
  119.8 1.4 copy-start
  121.2 79.3 %all-to-all-start.1 = ((bf16[128,64,128]{2,1,0:T(8,128)(2,1)}), bf16[128,64,128]{2,1,0:T(8,128)(2,1)}, u32[]{:S(2)}, u32[]{:S(2)}) async-start(bf16[128,64,128]{2,1,0:T(8,128)(2,1)} %to_coils.1), calls=%async_computation.1 | async-start | bytes 4194304 | tf_op jit(solution)/shard_map/all_to_all | solution.py:439
  138.1 17.3 %copy-start.13 = (s32[4,64]{1,0:T(4,128)S(1)}, s32[4,64]{1,0:T(4,128)}, u32[]{:S(2)}) copy-start(s32[4,64]{1,0:T(4,128)} %param.19) | copy-start | bytes 3076
  149.8 13.3 %collective-permute-start.5 = (bf16[2,64,512]{2,1,0:T(8,128)(2,1)}, bf16[2,64,512]{2,1,0:T(8,128)(2,1)S(1)}, u32[]{:S(2)}, u32[]{:S(2)}) collective-permute-start(bf16[2,64,512]{2,1,0:T(8,128)(2,1)} %image_g.1.mid), channel_id=1, source_target_pairs={{1,0},{2,1},{3,2},{4,3},{5,4},{6,5},{7,6},{8,7},{9,8},{10,9},{11,1... | collective-permute-start | bytes 393224 | tf_op jit(solution)/shard_map/ppermute | solution.py:445
  152.8 10.3 %collective-permute-start.4 = (bf16[2,64,512]{2,1,0:T(8,128)(2,1)}, bf16[2,64,512]{2,1,0:T(8,128)(2,1)S(1)}, u32[]{:S(2)}, u32[]{:S(2)}) collective-permute-start(bf16[2,64,512]{2,1,0:T(8,128)(2,1)} %image_g.1.mid), channel_id=1, source_target_pairs={{0,1},{1,2},{2,3},{3,4},{4,5},{5,6},{6,7},{7,8},{8,9},{9,10},{10,1... | collective-permute-start | bytes 393224 | tf_op jit(solution)/shard_map/ppermute | solution.py:445
  163.1 0.7 copy-start.7
  163.1 0.7 copy-start.8

commit v2 on v1

v2 whole, which is shorter than its diff:
```python
import math

import jax
import jax.numpy as jnp
import numpy as np
from jax import lax
from jax.experimental import pallas as pl
from jax.experimental.pallas import tpu as pltpu
from jax.sharding import PartitionSpec as P

MESH = pl.DeviceIdType.MESH
AXES = ("gy", "gz")
BF = jnp.bfloat16
F32 = jnp.float32
VMEM_LIMIT = 56 * 2**20
VM = pl.BlockSpec(memory_space=pltpu.VMEM)


def trig(length):
    index = np.arange(length, dtype=np.int64)
    angle = (index[:, None] * index[None, :] % length).astype(np.float64) * (2.0 * math.pi / length)
    factor = 1.0 / math.sqrt(length)
    return np.cos(angle) * factor, np.sin(angle) * factor


def as_bf16(array):
    return np.asarray(array, dtype=np.float32).astype(jnp.bfloat16)


def inverse_y_table(gy, rows):
    length = gy * rows
    cos, sin = trig(length)
    cos, sin = cos.reshape(gy, rows, length), sin.reshape(gy, rows, length)
    table = np.stack([np.stack([cos, sin], 2), np.stack([-sin, cos], 2)], 1)
    return as_bf16(table.reshape(2 * length, 2 * length))


def forward_y_table(gy, rows):
    length = gy * rows
    cos, sin = trig(length)
    cos, sin = cos.reshape(length, gy, rows), sin.reshape(length, gy, rows)
    table = np.stack([np.stack([cos, -sin], 2), np.stack([sin, cos], 2)], 0)
    return as_bf16(table.reshape(2 * length, 2 * length))


def z_table(length, inverse):
    cos, sin = trig(length)
    if inverse:
        table = np.block([[cos, -sin], [sin, cos]])
    else:
        table = np.block([[cos, sin], [-sin, cos]])
    return as_bf16(table)


def band_masks():
    zo, dz, j, zi = np.ogrid[0:8, 0:3, 0:3, 0:8]
    return (8 * (j - 1) + zi == zo + dz - 1).astype(np.float32)


def band_spread():
    hit = band_masks()
    eye = np.eye(18, dtype=np.float32)
    spread = np.einsum("odjz,kl->odkjlz", hit, eye)
    return as_bf16(spread.reshape(8, 54, 432))


def band_keep():
    hit = band_masks()
    keep = np.broadcast_to(hit.transpose(1, 0, 2, 3)[:, :, :, None, :], (3, 8, 3, 18, 8))
    return np.ascontiguousarray(keep.reshape(3, 8, 432)).astype(np.float32)


def band_gather():
    eye = np.eye(18, dtype=np.float32)
    return np.ascontiguousarray(np.broadcast_to(eye[None, :, None, :], (3, 18, 8, 18)).reshape(432, 18))


def out_spread():
    q, dz, zo = np.ogrid[0:10, 0:3, 0:8]
    hit = (q == zo + dz).astype(np.float32)
    eye = np.eye(18, dtype=np.float32)
    return as_bf16(np.einsum("qdz,kl->qdklz", hit, eye).reshape(10, 54, 144))


BATCH_A = 40


def shifted(value, dy):
    if dy == 1:
        return value
    lane = lax.broadcasted_iota(jnp.int32, value.shape, value.ndim - 1)
    if dy == 0:
        return jnp.where(lane == 0, 0.0, pltpu.roll(value, 1, value.ndim - 1))
    return jnp.where(lane == 511, 0.0, pltpu.roll(value, 511, value.ndim - 1))


def fill_columns(images, cols):
    cols[pl.ds(0, 144), :] = jnp.zeros((144, 512), BF)
    cols[pl.ds(1296, 144), :] = jnp.zeros((144, 512), BF)
    for dx, image in enumerate(images):
        parts = [image(i) for i in range(2)]
        for dy in range(3):
            pair = jnp.stack([shifted(part, dy).reshape(8, 8, 512) for part in parts], axis=1)
            pair = pair.reshape(8, 16, 512).astype(BF)
            for zb in range(8):
                cols[pl.ds((zb + 1) * 144 + (dy * 3 + dx) * 16, 16), :] = pair[zb]


def gather_terms(total, keep, gather):
    pieces = []
    total = total.reshape(8, 32, 432)
    for dz in range(3):
        kept = total[0] * keep[dz, 0:1, :]
        for zo in range(1, 8):
            kept = kept + total[zo] * keep[dz, zo : zo + 1, :]
        pieces.append(
            jnp.dot(kept, gather[...], preferred_element_type=F32, precision=lax.Precision.HIGHEST)
        )
    return pieces


def cascade(
    k_hbm, m_hbm, g_hbm, s_hbm, iy_hbm, fy_hbm, iz, fz, weight, w_in, bias, w_out, w_back, keep, gather,
    out_hbm, totals,
    kv, gv, mv, sens, iy, fy, stage, sk, sg, sf, rk, rg, rf,
    own_k, own_g, near_k, near_g, q_mid, q_send, q_near,
    cols, cols_g, hidden, slope, sum_in, sum_out, sum_b, first, second,
    load_sem, send_sem, recv_sem, store_sem,
):
    my_y, my_z = lax.axis_index("gy"), lax.axis_index("gz")
    me = my_y * 16 + my_z
    pos_x, pos_y, pos_z, pos_c = my_y % 4, my_y // 4 * 2 + my_z // 8, my_z // 2 % 4, my_z % 2
    left, right = (me + 127) % 128, (me + 1) % 128

    def pair(t):
        return (t // 16, t % 16)

    loads = [
        pltpu.make_async_copy(src, dst, load_sem.at[n])
        for n, (src, dst) in enumerate(
            [(k_hbm, kv), (g_hbm, gv), (iy_hbm, iy), (s_hbm, sens), (fy_hbm, fy), (m_hbm, mv)]
        )
    ]
    for load in loads:
        load.start()
    barrier = pltpu.get_barrier_semaphore()

    def greet(n):
        pl.semaphore_signal(barrier, inc=1, device_id=pair((me + n) % 128), device_id_type=MESH)

    def remote(src, dst, n, t):
        return pltpu.make_async_remote_copy(
            src_ref=src,
            dst_ref=dst,
            send_sem=send_sem.at[n],
            recv_sem=recv_sem.at[n],
            device_id=pair(t),
            device_id_type=MESH,
        )

    def target(i):
        n = i * 45 % 128
        x, y = (pos_x + n // 2 % 4) % 4, (pos_y + n // 8 % 4) % 4
        z, c = (pos_z + n // 32) % 4, (pos_c + n % 2) % 2
        return (y // 2 * 4 + x) * 16 + y % 2 * 8 + z * 2 + c

    def turn(source, index):
        depth, coil = index // 16, index % 16
        both = jnp.concatenate([source[0, coil, depth], source[1, coil, depth]], axis=0)
        stage[pl.ds(index, 128, stride=64), :] = both.astype(F32).T

    def block_of(t):
        return stage[pl.ds(pl.multiple_of(t * 64, 64), 64), :].astype(BF)

    loads[0].wait()
    turn(kv, 0)
    greet(64)

    def turn_k(index, carry):
        turn(kv, index)
        greet(index)
        greet(index + 64)
        return carry

    lax.fori_loop(1, 64, turn_k, 0)
    pl.semaphore_wait(barrier, 127)
    rk[me] = block_of(me)

    def send_k(i, carry):
        t = target(i)
        sk[t] = block_of(t)
        remote(sk.at[t], rk.at[me], 0, t).start()
        return carry

    lax.fori_loop(1, 128, send_k, 0)
    loads[1].wait()

    def turn_g(index, carry):
        turn(gv, index)
        return carry

    lax.fori_loop(0, 64, turn_g, 0, unroll=2)
    rg[me] = block_of(me)

    def send_g(i):
        t = target(i)
        remote(sg.at[t], rg.at[me], 1, t).start()

    def first_g(i, carry):
        t = target(i)
        sg[t] = block_of(t)
        send_g(i)
        return carry

    def keep_g(i, carry):
        t = target(i)
        sg[t] = block_of(t)
        return carry

    lax.fori_loop(1, BATCH_A, first_g, 0)
    lax.fori_loop(BATCH_A, 128, keep_g, 0, unroll=2)

    def wait_blocks(sent, got, n):
        every = pltpu.make_async_remote_copy(
            src_ref=sent.at[pl.ds(0, 127)],
            dst_ref=got.at[pl.ds(0, 127)],
            send_sem=send_sem.at[n],
            recv_sem=recv_sem.at[n],
            device_id=pair(right),
            device_id_type=MESH,
        )
        every.wait_send()
        every.wait_recv()

    def to_image(tiles, image):
        def rows(m, carry):
            lines = jnp.concatenate(
                [tiles[pl.ds(gy * 16 + m * 4, 4)].reshape(256, 128) for gy in range(8)], axis=1
            )
            done = jnp.dot(lines, iy[...], preferred_element_type=F32)
            for lt in range(8):
                span = pl.ds(pl.multiple_of(lt * 1024 + m * 256, 256), 256)
                stage[span, :] = done[:, lt * 128 : lt * 128 + 128]
            return carry

        lax.fori_loop(0, 4, rows, 0)

        def coil(c, carry):
            real, imag = carry
            lines = [stage[pl.ds(lt * 1024 + c, 64, stride=16), :].astype(BF) for lt in range(8)]
            lines = [jnp.concatenate(lines[4 * p : 4 * p + 4], axis=1) for p in range(2)]
            done = jnp.dot(iz[...], jnp.concatenate(lines, axis=0), preferred_element_type=F32)
            c_r, c_i = done[:64], done[64:]
            s_r, s_i = sens[0, 0, c].astype(F32), sens[1, 0, c].astype(F32)
            return real + (s_r * c_r + s_i * c_i), imag + (s_r * c_i - s_i * c_r)

        zero = jnp.zeros((64, 512), F32)
        real, imag = lax.fori_loop(0, 16, coil, (zero, zero))
        image[0] = real.astype(BF)
        image[1] = imag.astype(BF)

    def to_neighbours(up, down, near, n):
        copies = [remote(up, near.at[0], n, right), remote(down, near.at[1], n + 1, left)]
        for copy in copies:
            copy.start()
        return copies

    def beside(near, side, i):
        inside = me > 0 if side == 0 else me < 127
        return jnp.where(inside, near[side, i].astype(F32), 0.0)

    def three(own, near):
        return (
            lambda i: beside(near, 0, i),
            lambda i: own[i].astype(F32),
            lambda i: beside(near, 1, i),
        )

    loads[2].wait()
    loads[3].wait()
    wait_blocks(sk, rk, 0)
    to_image(rk, own_k)
    for copy in to_neighbours(own_k, own_k, near_k, 3):
        copy.wait()

    fill_columns(three(own_k, near_k), cols)
    hidden[pl.ds(0, 32), :] = jnp.zeros((32, 512), BF)
    hidden[pl.ds(65 * 32, 32), :] = jnp.zeros((32, 512), BF)

    def conv_in_block(zb, carry):
        for i in range(5):
            send_g(BATCH_A + zb * 5 + i)
        window = cols[pl.ds(pl.multiple_of(zb * 144, 16), 432), :]
        pre = jnp.dot(w_in[...], window, preferred_element_type=F32) + bias[...]
        sig = jax.nn.sigmoid(pre)
        hidden[pl.ds(pl.multiple_of(zb * 256 + 32, 32), 256), :] = (pre * sig).astype(BF)
        slope[pl.ds(pl.multiple_of(zb * 256, 256), 256), :] = sig * (1.0 + pre * (1.0 - sig))
        return carry

    lax.fori_loop(0, 8, conv_in_block, 0)

    def conv_out_block(zb, carry):
        window = hidden[pl.ds(pl.multiple_of(zb * 256, 256), 320), :]
        terms = jnp.dot(w_out[...], window, preferred_element_type=F32).reshape(18, 8, 512)
        rows = pl.ds(pl.multiple_of(zb * 8, 8), 8)
        for dx in range(3):
            for o in range(2):
                base = (dx * 2 + o) * 3
                total = shifted(terms[base], 0) + terms[base + 1] + shifted(terms[base + 2], 2)
                q_mid[dx, o, rows, :] = total
        return carry

    lax.fori_loop(0, 8, conv_out_block, 0)
    q_send[0] = q_mid[0].astype(BF)
    q_send[1] = q_mid[2].astype(BF)
    for copy in to_neighbours(q_send.at[0], q_send.at[1], q_near, 5):
        copy.wait()

    r_r, r_i = [
        (beside(q_near, 0, o) + q_mid[1, o] + beside(q_near, 1, o)).astype(BF).astype(F32)
        for o in range(2)
    ]

    def spread(c, carry):
        for i in range(3):
            send_g(BATCH_A + 40 + c * 3 + i)
        s_r, s_i = sens[0, 0, c].astype(F32), sens[1, 0, c].astype(F32)
        lines = jnp.concatenate([s_r * r_r - s_i * r_i, s_r * r_i + s_i * r_r], axis=0).astype(BF)
        done = jnp.dot(fz[...], lines, preferred_element_type=F32)
        for lt in range(8):
            p, lane = lt // 4, lt % 4 * 128
            stage[pl.ds(lt * 1024 + c, 64, stride=16), :] = done[p * 64 : p * 64 + 64, lane : lane + 128]
        return carry

    lax.fori_loop(0, 16, spread, 0)
    loads[4].wait()

    def send_f(step, carry):
        m = (step + my_z // 4) % 4
        lines = [stage[pl.ds(pl.multiple_of(lt * 1024 + m * 256, 256), 256), :] for lt in range(8)]
        lines = jnp.concatenate([part.astype(BF) for part in lines], axis=1)
        done = jnp.dot(lines, fy[...], preferred_element_type=F32).astype(BF)
        for gy in range(8):
            sf[pl.ds(gy * 16 + m * 4, 4)] = done[:, gy * 128 : gy * 128 + 128].reshape(4, 64, 128)

        def start(j, inner):
            t = (my_y + j % 8) % 8 * 16 + m * 4 + (my_z + j // 8) % 4

            @pl.when(t != me)
            def _():
                remote(sf.at[t], rf.at[me], 2, t).start()

            return inner

        lax.fori_loop(0, 32, start, 0)
        return carry

    lax.fori_loop(0, 4, send_f, 0)
    rf[me] = sf[me]

    wait_blocks(sg, rg, 1)
    to_image(rg, own_g)
    for copy in to_neighbours(own_g, own_g, near_g, 7):
        copy.wait()
    fill_columns(three(own_g, near_g), cols_g)
    sum_in[...] = jnp.zeros_like(sum_in)
    sum_out[...] = jnp.zeros_like(sum_out)
    sum_b[...] = jnp.zeros_like(sum_b)
    nt = (((1,), (1,)), ((), ()))

    def back_block(zb, carry):
        span = pl.ds(pl.multiple_of(zb * 144, 16), 432)
        window_g = cols_g[span, :]
        back = jnp.dot(w_back[...], window_g, preferred_element_type=F32)
        back = (back * slope[pl.ds(pl.multiple_of(zb * 256, 256), 256), :]).astype(BF)
        sum_in[...] += lax.dot_general(back, cols[span, :], nt, preferred_element_type=F32)
        held = hidden[pl.ds(pl.multiple_of(zb * 256 + 32, 32), 256), :]
        sum_out[...] += lax.dot_general(held, window_g, nt, preferred_element_type=F32)
        wide = back.astype(F32)
        sum_b[...] += wide[:, :128] + wide[:, 128:256] + wide[:, 256:384] + wide[:, 384:]
        return carry

    lax.fori_loop(0, 8, back_block, 0)
    bias_sum = jnp.sum(sum_b[...].reshape(8, 32, 128), axis=0)
    bias_sum = jnp.sum(bias_sum, axis=1, keepdims=True)
    pieces = gather_terms(sum_in[...], keep, gather) + gather_terms(sum_out[...], keep, gather)
    pieces.append(jnp.broadcast_to(bias_sum, (32, 20)))

    def share(buffer, mine, count, n, device):
        def start(step, carry):
            remote(buffer.at[mine], buffer.at[mine], n, device((mine + step) % count)).start()
            return carry

        lax.fori_loop(1, count, start, 0)

    def collect(buffer, count, n):
        every = pltpu.make_async_remote_copy(
            src_ref=buffer.at[pl.ds(0, count - 1)],
            dst_ref=buffer.at[pl.ds(0, count - 1)],
            send_sem=send_sem.at[n],
            recv_sem=recv_sem.at[n],
            device_id=pair(right),
            device_id_type=MESH,
        )
        every.wait_send()
        every.wait_recv()
        total = buffer[0]
        for index in range(1, count):
            total = total + buffer[index]
        return total

    first[my_z] = jnp.concatenate(pieces, axis=1)
    share(first, my_z, 16, 9, lambda to: my_y * 16 + to)

    loads[5].wait()
    wait_blocks(sf, rf, 2)

    def widen(x, carry):
        stage[pl.ds(pl.multiple_of(x * 64, 64), 64), :] = rf[x].astype(F32)
        return carry

    lax.fori_loop(0, 128, widen, 0, unroll=4)
    second[my_y] = collect(first, 16, 9)
    share(second, my_y, 8, 10, lambda to: to * 16 + my_z)

    def finish(index, carry):
        depth, coil = index // 16, index % 16
        both = stage[pl.ds(index, 128, stride=64), :].T
        part_of = weight[depth]
        for part in range(2):
            current = kv[part, coil, depth].astype(F32)
            other = mv[part, coil, depth].astype(F32)
            refine = both[part * 64 : part * 64 + 64]
            kv[part, coil, depth] = (current - part_of * (current - other) + refine).astype(BF)
        return carry

    stores = []
    for depth in range(4):
        lax.fori_loop(depth * 16, depth * 16 + 16, finish, 0, unroll=2)
        stores.append(
            pltpu.make_async_copy(kv.at[:, :, depth], out_hbm.at[:, :, depth], store_sem.at[depth])
        )
        stores[-1].start()
    totals[...] = collect(second, 8, 10)
    for store in stores:
        store.wait()


def run_cascade(*operands):
    blocks = pltpu.VMEM((128, 64, 128), BF)
    tile = pltpu.VMEM((2, 16, 4, 64, 128), BF)
    image = pltpu.VMEM((2, 64, 512), BF)
    near = pltpu.VMEM((2, 2, 64, 512), BF)
    table = pltpu.VMEM((1024, 1024), BF)
    hbm = pl.BlockSpec(memory_space=pl.ANY)
    return pl.pallas_call(
        cascade,
        out_shape=(
            jax.ShapeDtypeStruct((2, 16, 4, 64, 128), BF),
            jax.ShapeDtypeStruct((32, 128), F32),
        ),
        in_specs=[hbm] * 6 + [VM] * 9,
        out_specs=(hbm, VM),
        scratch_shapes=[
            tile, tile, tile,
            pltpu.VMEM((2, 1, 16, 64, 512), BF),
            table, table,
            pltpu.VMEM((8192, 128), F32),
            blocks, blocks, blocks, blocks, blocks, blocks,
            image, image, near, near,
            pltpu.VMEM((3, 2, 64, 512), F32),
            near, near,
            pltpu.VMEM((1440, 512), BF),
            pltpu.VMEM((1440, 512), BF),
            pltpu.VMEM((66 * 32, 512), BF),
            pltpu.VMEM((2048, 512), F32),
            pltpu.VMEM((256, 432), F32),
            pltpu.VMEM((256, 432), F32),
            pltpu.VMEM((256, 128), F32),
            pltpu.VMEM((16, 32, 128), F32),
            pltpu.VMEM((8, 32, 128), F32),
            pltpu.SemaphoreType.DMA((6,)),
            pltpu.SemaphoreType.DMA((11,)),
            pltpu.SemaphoreType.DMA((11,)),
            pltpu.SemaphoreType.DMA((4,)),
        ],
        compiler_params=pltpu.CompilerParams(
            collective_id=0, has_side_effects=True, vmem_limit_bytes=VMEM_LIMIT
        ),
        name="cascade",
    )(*operands)


def on_device(
    kspace, measured, sample_mask, step_size, coil_field, conv_in, bias_in, conv_out, cotangent
):
    count_y, count_z = lax.axis_size("gy"), lax.axis_size("gz")
    row_tile, x_cells, depth_tile = kspace.shape[3], kspace.shape[4], kspace.shape[2]
    inverse_y = jnp.asarray(inverse_y_table(count_y, row_tile))
    forward_y = jnp.asarray(forward_y_table(count_y, row_tile))
    inverse_z = jnp.asarray(z_table(count_z * depth_tile, True))
    forward_z = jnp.asarray(z_table(count_z * depth_tile, False))
    spread = jnp.asarray(band_spread())
    keep = jnp.asarray(band_keep())
    gather = jnp.asarray(band_gather())
    spread_out = jnp.asarray(out_spread())

    flat_in = conv_in.transpose(0, 2, 3, 4, 1).reshape(32, 54)
    w_in = jnp.einsum("ok,zkc->zoc", flat_in, spread).reshape(256, 432)
    flat_back = conv_out[:, :, ::-1, ::-1, ::-1].transpose(1, 2, 3, 4, 0).reshape(32, 54)
    w_back = jnp.einsum("ok,zkc->zoc", flat_back, spread).reshape(256, 432)
    flat_out = conv_out.transpose(1, 2, 4, 0, 3).reshape(32, 54)
    w_out = jnp.einsum("ik,qkr->rqi", flat_out, spread_out).reshape(144, 320)
    bias = jnp.tile(bias_in, 8)[:, None]
    weight = jnp.broadcast_to(
        (step_size[0] * sample_mask.astype(F32))[:, :, None], (depth_tile, row_tile, x_cells)
    )

    kspace_next, totals = run_cascade(
        kspace, measured, cotangent, coil_field, inverse_y, forward_y, inverse_z, forward_z,
        weight, w_in, bias, w_out, w_back, keep, gather,
    )

    norm = 1.0 / math.sqrt(x_cells * row_tile * count_y * depth_tile * count_z)
    totals = totals * norm
    grad_in = totals[:, :54].reshape(32, 3, 3, 3, 2).transpose(0, 4, 1, 2, 3)
    grad_out = totals[:, 54:108].reshape(32, 3, 3, 3, 2).transpose(4, 0, 1, 2, 3)
    grad_out = grad_out[:, :, ::-1, ::-1, ::-1]
    return kspace_next, grad_in, totals[:, 108], grad_out


def solution(mesh):
    tile = P(None, None, "gz", "gy", None)
    in_specs = (
        tile,
        tile,
        P("gz", "gy"),
        P(),
        P(None, AXES, None, None, None),
        P(),
        P(),
        P(),
        tile,
    )
    out_specs = (tile, P(), P(), P())
    return jax.shard_map(
        on_device, mesh=mesh, in_specs=in_specs, out_specs=out_specs, check_vma=False
    )
```

time: 211 us -> 161 us (0.76)
  starting transfers between devices: 48.1 us -> 0 us
  waiting for transfers between devices: 42.3 us -> 0 us
  Pallas kernels: 106 us -> 143 us
    pallas_call x9 -> x1, Pallas kernels: 106 us -> 143 us  [run_cascade(): pl.pallas_call(cascade, out_shape=(jax.ShapeDtypeStruct((2, 16, 4, 64, 12...]
    all_to_all x3 -> x0, starting transfers between devices: 30.8 us -> none  [exchange(): return lax.all_to_all(blocks, AXES, split_axis=0, concat_axis=0, tiled=True)]
    all_to_all x3 -> x0, waiting for transfers between devices: 21.9 us -> none  [exchange(): return lax.all_to_all(blocks, AXES, split_axis=0, concat_axis=0, tiled=True)]
    ppermute x6 -> x0, waiting for transfers between devices: 20.4 us -> none  [the longest x4 14.5 us: neighbours(): return (lax.ppermute(image, AXES, up), lax.ppermute(image, AXES, down))]
    ppermute x6 -> x0, starting transfers between devices: 17.3 us -> none  [the longest x4 11.1 us: neighbours(): return (lax.ppermute(image, AXES, up), lax.ppermute(image, AXES, down))]
    unnamed x31 -> x4, local copies, waits for them, and re-layouts: 4.88 us -> 3.91 us
  transfers between devices with their start and end apart: 9 -> 0, of which waited for: 5 -> 0; matrix products, arithmetic and copies ran while one was open for 3% -> 0% of each run, Pallas kernels for 42% -> 0%
where the time goes in v2:
time: 161 us; the launch traced here: 160 us
  Pallas kernels  143 us (89%)
  local copies, waits for them, and re-layouts  10.6 us (7%)
  matrix products  4.21 us (3%)
    pallas_call x1, Pallas kernels, run_cascade(): pl.pallas_call(cascade, out_shape=(jax.ShapeDtypeStruct((2, 16, 4, 64, 12...  143 us
    unnamed x4, local copies, waits for them, and re-layouts  3.91 us

profile of v2, /device:TPU:1, one launch (start us, length us, event | category | flops | bytes accessed | tf_op | source)
XLA Modules:
  0.0 160.3 jit_solution(16086659042636215374)
XLA Ops:
  0.6 0.0 copy-start
  1.3 0.7 convert_multiply_fusion
  2.0 0.7 tile.2
  2.7 0.7 reverse_bitcast_fusion
  3.4 0.7 copy.25
  4.2 0.7 copy.27
  4.9 0.8 broadcast_in_dim_tile.4.bias
  5.7 0.8 broadcast_in_dim.2.weight
  6.5 1.2 fusion
  7.7 0.8 copy.31.w_out
  8.4 2.0 %fusion.4 = bf16[8,432,32]{1,2,0:T(8,128)(2,1)} fusion(bf16[8,54,432]{2,1,0:T(8,128)(2,1)} %constant.33, bf16[32,54]{0,1:T(8,128)(2,1)S(1)} %reshape.42), kind=kOutput, calls=%fused_computation.5 | convolution fusion | flops 11943936 | bytes 597888 | tf_op jit(solution)/shard_map/ok,zkc->zoc/dot_general | solution.py:509
  10.4 0.0 copy-done
  10.4 1.0 fusion.2
  11.5 142.7 %cascade.1 = (bf16[2,16,4,64,128]{4,3,2,1,0:T(8,128)(2,1)}, f32[32,128]{1,0:T(8,128)}) custom-call(bf16[2,16,4,64,128]{4,3,2,1,0:T(8,128)(2,1)} %k_hbm.1, bf16[2,16,4,64,128]{4,3,2,1,0:T(8,128)(2,1)} %m_hbm.1, bf16[2,16,4,64,128]{4,3,2,1,0:T(8,128)(2,1)} %g_hbm.1, bf16[2,1,16,64,512]{4,3,2,1,0:T(8,128)(2,1)} %s_hbm.1, ...), custom_call_target="tpu_custom_call" | custom-call | tf_op jit(solution)/shard_map/cascade/pallas_call | solution.py:456
  154.1 0.7 broadcast_multiply_fusion
  154.9 0.7 slice_reduce_fusion
  155.5 0.1 fusion.6
  155.6 0.1 copy.33
  155.7 0.6 rev.7
  156.4 0.1 copy.32
  156.4 0.6 reshape.40
  157.1 3.2 %copy.42 = bf16[2,16,4,64,128]{4,3,2,1,0:T(8,128)(2,1)} copy(bf16[2,16,4,64,128]{4,3,2,1,0:T(8,128)(2,1)} %get-tuple-element.14) | data formatting | bytes 4194304
  (4 shorter events, 0.1 us)
Async XLA Ops:
  0.6 9.8 %copy-start = (bf16[8,54,432]{2,1,0:T(8,128)(2,1)S(1)}, bf16[8,54,432]{2,1,0:T(8,128)(2,1)}, u32[]{:S(2)}) copy-start(bf16[8,54,432]{2,1,0:T(8,128)(2,1)} %constant.22.clone) | copy-start | bytes 1119748

commit v3 on v2

--- a/solution.py
+++ b/solution.py
@@ -1,3 +1,4 @@
+import functools
 import math
 
 import jax
@@ -70,19 +71,27 @@
     return np.ascontiguousarray(keep.reshape(3, 8, 432)).astype(np.float32)
 
 
+def band_spread_flipped():
+    spread = band_spread().reshape(8, 3, 3, 3, 2, 432)
+    return np.ascontiguousarray(spread[:, ::-1, ::-1, ::-1].reshape(8, 54, 432))
+
+
 def band_gather():
     eye = np.eye(18, dtype=np.float32)
-    return np.ascontiguousarray(np.broadcast_to(eye[None, :, None, :], (3, 18, 8, 18)).reshape(432, 18))
+    both = np.stack([eye, eye.reshape(18, 3, 3, 2)[:, ::-1, ::-1].reshape(18, 18)])
+    both = np.broadcast_to(both[:, None, :, None, :], (2, 3, 18, 8, 18))
+    return np.ascontiguousarray(both.reshape(2, 432, 18))
 
 
 def out_spread():
     q, dz, zo = np.ogrid[0:10, 0:3, 0:8]
     hit = (q == zo + dz).astype(np.float32)
-    eye = np.eye(18, dtype=np.float32)
-    return as_bf16(np.einsum("qdz,kl->qdklz", hit, eye).reshape(10, 54, 144))
-
-
-BATCH_A = 40
+    three, two = np.eye(3, dtype=np.float32), np.eye(2, dtype=np.float32)
+    spread = np.einsum("qdz,yY,xX,oO->qdyxoXOYz", hit, three, three, two)
+    return as_bf16(spread.reshape(10, 54, 144))
+
+
+BATCH = 64
 
 
 def shifted(value, dy):
@@ -106,25 +115,28 @@
                 cols[pl.ds((zb + 1) * 144 + (dy * 3 + dx) * 16, 16), :] = pair[zb]
 
 
-def gather_terms(total, keep, gather):
+def gather_terms(total, keep, gather, order):
     pieces = []
     total = total.reshape(8, 32, 432)
-    for dz in range(3):
+    for dz in order:
         kept = total[0] * keep[dz, 0:1, :]
         for zo in range(1, 8):
             kept = kept + total[zo] * keep[dz, zo : zo + 1, :]
         pieces.append(
-            jnp.dot(kept, gather[...], preferred_element_type=F32, precision=lax.Precision.HIGHEST)
+            jnp.dot(kept, gather, preferred_element_type=F32, precision=lax.Precision.HIGHEST)
         )
     return pieces
 
 
 def cascade(
-    k_hbm, m_hbm, g_hbm, s_hbm, iy_hbm, fy_hbm, iz, fz, weight, w_in, bias, w_out, w_back, keep, gather,
-    out_hbm, totals,
+    norm,
+    k_hbm, m_hbm, g_hbm, s_hbm, iy_hbm, fy_hbm, spread_in_hbm, spread_back_hbm, spread_out_hbm,
+    iz, fz, mask, step, flat_in, bias, flat_out, keep, gather,
+    out_hbm, grad_in, grad_bias, grad_out,
     kv, gv, mv, sens, iy, fy, stage, sk, sg, sf, rk, rg, rf,
     own_k, own_g, near_k, near_g, q_mid, q_send, q_near,
     cols, cols_g, hidden, slope, sum_in, sum_out, sum_b, first, second,
+    weight, bias_cols, w_in, w_back, w_out, spread_in, spread_back, spread_out,
     load_sem, send_sem, recv_sem, store_sem,
 ):
     my_y, my_z = lax.axis_index("gy"), lax.axis_index("gz")
@@ -133,20 +145,24 @@
     left, right = (me + 127) % 128, (me + 1) % 128
 
     def pair(t):
-        return (t // 16, t % 16)
+        return (lax.div(t, 16), lax.rem(t, 16))
 
     loads = [
         pltpu.make_async_copy(src, dst, load_sem.at[n])
         for n, (src, dst) in enumerate(
-            [(k_hbm, kv), (g_hbm, gv), (iy_hbm, iy), (s_hbm, sens), (fy_hbm, fy), (m_hbm, mv)]
+            [(k_hbm, kv), (g_hbm, gv), (iy_hbm, iy), (s_hbm, sens), (fy_hbm, fy), (m_hbm, mv),
+             (spread_in_hbm, spread_in), (spread_back_hbm, spread_back), (spread_out_hbm, spread_out)]
         )
     ]
     for load in loads:
         load.start()
     barrier = pltpu.get_barrier_semaphore()
 
-    def greet(n):
-        pl.semaphore_signal(barrier, inc=1, device_id=pair((me + n) % 128), device_id_type=MESH)
+    def greet(n, carry):
+        pl.semaphore_signal(barrier, inc=1, device_id=pair(lax.rem(me + n, 128)), device_id_type=MESH)
+        return carry
+
+    lax.fori_loop(1, 128, greet, 0)
 
     def remote(src, dst, n, t):
         return pltpu.make_async_remote_copy(
@@ -159,32 +175,24 @@
         )
 
     def target(i):
-        n = i * 45 % 128
-        x, y = (pos_x + n // 2 % 4) % 4, (pos_y + n // 8 % 4) % 4
-        z, c = (pos_z + n // 32) % 4, (pos_c + n % 2) % 2
-        return (y // 2 * 4 + x) * 16 + y % 2 * 8 + z * 2 + c
+        n = lax.rem(i * 45, 128)
+        x = lax.rem(pos_x + lax.rem(lax.div(n, 2), 4), 4)
+        y = lax.rem(pos_y + lax.rem(lax.div(n, 8), 4), 4)
+        z = lax.rem(pos_z + lax.div(n, 32), 4)
+        c = lax.rem(pos_c + lax.rem(n, 2), 2)
+        return (lax.div(y, 2) * 4 + x) * 16 + lax.rem(y, 2) * 8 + z * 2 + c
 
     def turn(source, index):
         depth, coil = index // 16, index % 16
         both = jnp.concatenate([source[0, coil, depth], source[1, coil, depth]], axis=0)
-        stage[pl.ds(index, 128, stride=64), :] = both.astype(F32).T
+        stage[pl.ds(index, 128, stride=64), :] = both.T.astype(F32)
 
     def block_of(t):
         return stage[pl.ds(pl.multiple_of(t * 64, 64), 64), :].astype(BF)
 
-    loads[0].wait()
-    turn(kv, 0)
-    greet(64)
-
     def turn_k(index, carry):
         turn(kv, index)
-        greet(index)
-        greet(index + 64)
-        return carry
-
-    lax.fori_loop(1, 64, turn_k, 0)
-    pl.semaphore_wait(barrier, 127)
-    rk[me] = block_of(me)
+        return carry
 
     def send_k(i, carry):
         t = target(i)
@@ -192,24 +200,20 @@
         remote(sk.at[t], rk.at[me], 0, t).start()
         return carry
 
+    loads[0].wait()
+    lax.fori_loop(0, 64, turn_k, 0, unroll=2)
+    pl.semaphore_wait(barrier, 127)
+    rk[me] = block_of(me)
     lax.fori_loop(1, 128, send_k, 0)
-    loads[1].wait()
 
     def turn_g(index, carry):
         turn(gv, index)
         return carry
-
-    lax.fori_loop(0, 64, turn_g, 0, unroll=2)
-    rg[me] = block_of(me)
-
-    def send_g(i):
-        t = target(i)
-        remote(sg.at[t], rg.at[me], 1, t).start()
 
     def first_g(i, carry):
         t = target(i)
         sg[t] = block_of(t)
-        send_g(i)
+        remote(sg.at[t], rg.at[me], 1, t).start()
         return carry
 
     def keep_g(i, carry):
@@ -217,8 +221,41 @@
         sg[t] = block_of(t)
         return carry
 
-    lax.fori_loop(1, BATCH_A, first_g, 0)
-    lax.fori_loop(BATCH_A, 128, keep_g, 0, unroll=2)
+    def later_g(i, carry):
+        t = target(i)
+        remote(sg.at[t], rg.at[me], 1, t).start()
+        return carry
+
+    loads[1].wait()
+    lax.fori_loop(0, 64, turn_g, 0, unroll=2)
+    rg[me] = block_of(me)
+    lax.fori_loop(1, BATCH, first_g, 0)
+    lax.fori_loop(BATCH, 128, keep_g, 0, unroll=2)
+
+    for n in (6, 7, 8):
+        loads[n].wait()
+    contract = (((0,), (0,)), ((), ()))
+    for zo in range(8):
+        rows = pl.ds(zo * 32, 32)
+        band = lax.dot_general(flat_in[...], spread_in[zo], contract, preferred_element_type=F32)
+        w_in[rows, :] = band.astype(BF)
+        band = lax.dot_general(flat_out[...], spread_back[zo], contract, preferred_element_type=F32)
+        w_back[rows, :] = band.astype(BF)
+    bands = [
+        lax.dot_general(spread_out[q], flat_out[...], contract, preferred_element_type=F32)
+        for q in range(10)
+    ]
+    w_out[...] = jnp.concatenate(bands, axis=1).astype(BF)
+
+    def upright(row):
+        return jnp.broadcast_to(row, (128, 128)).T
+
+    bias_rows = upright(jnp.concatenate([bias[...]] * 4, axis=1))[:32]
+    for zo in range(8):
+        bias_cols[pl.ds(zo * 32, 32), :] = bias_rows
+    for depth in range(4):
+        row = mask[pl.ds(depth, 1), :].astype(F32) * step[...]
+        weight[depth] = upright(jnp.concatenate([row, row], axis=1))[:64]
 
     def wait_blocks(sent, got, n):
         every = pltpu.make_async_remote_copy(
@@ -245,19 +282,32 @@
 
         lax.fori_loop(0, 4, rows, 0)
 
-        def coil(c, carry):
-            real, imag = carry
-            lines = [stage[pl.ds(lt * 1024 + c, 64, stride=16), :].astype(BF) for lt in range(8)]
-            lines = [jnp.concatenate(lines[4 * p : 4 * p + 4], axis=1) for p in range(2)]
-            done = jnp.dot(iz[...], jnp.concatenate(lines, axis=0), preferred_element_type=F32)
-            c_r, c_i = done[:64], done[64:]
-            s_r, s_i = sens[0, 0, c].astype(F32), sens[1, 0, c].astype(F32)
-            return real + (s_r * c_r + s_i * c_i), imag + (s_r * c_i - s_i * c_r)
-
-        zero = jnp.zeros((64, 512), F32)
-        real, imag = lax.fori_loop(0, 16, coil, (zero, zero))
-        image[0] = real.astype(BF)
-        image[1] = imag.astype(BF)
+        for chunk in range(4):
+            lane = pl.ds(chunk * 128, 128)
+
+            def coils(step_c, carry):
+                real, imag = carry
+                lines = []
+                for c in (2 * step_c, 2 * step_c + 1):
+                    halves = [
+                        stage[pl.ds((p * 4 + chunk) * 1024 + c, 64, stride=16), :] for p in range(2)
+                    ]
+                    lines.append(jnp.concatenate(halves, axis=0).astype(BF))
+                done = jnp.dot(
+                    iz[...], jnp.concatenate(lines, axis=1), preferred_element_type=F32
+                )
+                for k in range(2):
+                    c = 2 * step_c + k
+                    c_r, c_i = done[:64, k * 128 : k * 128 + 128], done[64:, k * 128 : k * 128 + 128]
+                    s_r, s_i = sens[0, 0, c, :, lane].astype(F32), sens[1, 0, c, :, lane].astype(F32)
+                    real = real + (s_r * c_r + s_i * c_i)
+                    imag = imag + (s_r * c_i - s_i * c_r)
+                return real, imag
+
+            zero = jnp.zeros((64, 128), F32)
+            real, imag = lax.fori_loop(0, 8, coils, (zero, zero), unroll=2)
+            image[0, :, lane] = real.astype(BF)
+            image[1, :, lane] = imag.astype(BF)
 
     def to_neighbours(up, down, near, n):
         copies = [remote(up, near.at[0], n, right), remote(down, near.at[1], n + 1, left)]
@@ -280,7 +330,9 @@
     loads[3].wait()
     wait_blocks(sk, rk, 0)
     to_image(rk, own_k)
-    for copy in to_neighbours(own_k, own_k, near_k, 3):
+    copies = to_neighbours(own_k, own_k, near_k, 3)
+    lax.fori_loop(BATCH, 128, later_g, 0)
+    for copy in copies:
         copy.wait()
 
     fill_columns(three(own_k, near_k), cols)
@@ -288,10 +340,9 @@
     hidden[pl.ds(65 * 32, 32), :] = jnp.zeros((32, 512), BF)
 
     def conv_in_block(zb, carry):
-        for i in range(5):
-            send_g(BATCH_A + zb * 5 + i)
         window = cols[pl.ds(pl.multiple_of(zb * 144, 16), 432), :]
-        pre = jnp.dot(w_in[...], window, preferred_element_type=F32) + bias[...]
+        pre = jnp.dot(w_in[...], window, preferred_element_type=F32)
+        pre = pre + jnp.concatenate([bias_cols[...]] * 4, axis=1)
         sig = jax.nn.sigmoid(pre)
         hidden[pl.ds(pl.multiple_of(zb * 256 + 32, 32), 256), :] = (pre * sig).astype(BF)
         slope[pl.ds(pl.multiple_of(zb * 256, 256), 256), :] = sig * (1.0 + pre * (1.0 - sig))
@@ -313,26 +364,35 @@
     lax.fori_loop(0, 8, conv_out_block, 0)
     q_send[0] = q_mid[0].astype(BF)
     q_send[1] = q_mid[2].astype(BF)
-    for copy in to_neighbours(q_send.at[0], q_send.at[1], q_near, 5):
+    q_copies = to_neighbours(q_send.at[0], q_send.at[1], q_near, 5)
+
+    wait_blocks(sg, rg, 1)
+    to_image(rg, own_g)
+    g_copies = to_neighbours(own_g, own_g, near_g, 7)
+    for copy in q_copies:
         copy.wait()
 
-    r_r, r_i = [
-        (beside(q_near, 0, o) + q_mid[1, o] + beside(q_near, 1, o)).astype(BF).astype(F32)
-        for o in range(2)
-    ]
-
-    def spread(c, carry):
-        for i in range(3):
-            send_g(BATCH_A + 40 + c * 3 + i)
-        s_r, s_i = sens[0, 0, c].astype(F32), sens[1, 0, c].astype(F32)
-        lines = jnp.concatenate([s_r * r_r - s_i * r_i, s_r * r_i + s_i * r_r], axis=0).astype(BF)
-        done = jnp.dot(fz[...], lines, preferred_element_type=F32)
-        for lt in range(8):
-            p, lane = lt // 4, lt % 4 * 128
-            stage[pl.ds(lt * 1024 + c, 64, stride=16), :] = done[p * 64 : p * 64 + 64, lane : lane + 128]
-        return carry
-
-    lax.fori_loop(0, 16, spread, 0)
+    for o in range(2):
+        total = beside(q_near, 0, o) + q_mid[1, o] + beside(q_near, 1, o)
+        q_mid[0, o] = total.astype(BF).astype(F32)
+    for chunk in range(4):
+        lane = pl.ds(chunk * 128, 128)
+        r_r, r_i = q_mid[0, 0, :, lane], q_mid[0, 1, :, lane]
+
+        def spread(step_c, carry):
+            lines = []
+            for c in (2 * step_c, 2 * step_c + 1):
+                s_r, s_i = sens[0, 0, c, :, lane].astype(F32), sens[1, 0, c, :, lane].astype(F32)
+                both = [s_r * r_r - s_i * r_i, s_r * r_i + s_i * r_r]
+                lines.append(jnp.concatenate(both, axis=0).astype(BF))
+            done = jnp.dot(fz[...], jnp.concatenate(lines, axis=1), preferred_element_type=F32)
+            for k in range(2):
+                for p in range(2):
+                    rows = pl.ds((p * 4 + chunk) * 1024 + 2 * step_c + k, 64, stride=16)
+                    stage[rows, :] = done[p * 64 : p * 64 + 64, k * 128 : k * 128 + 128]
+            return carry
+
+        lax.fori_loop(0, 8, spread, 0, unroll=2)
     loads[4].wait()
 
     def send_f(step, carry):
@@ -358,9 +418,7 @@
     lax.fori_loop(0, 4, send_f, 0)
     rf[me] = sf[me]
 
-    wait_blocks(sg, rg, 1)
-    to_image(rg, own_g)
-    for copy in to_neighbours(own_g, own_g, near_g, 7):
+    for copy in g_copies:
         copy.wait()
     fill_columns(three(own_g, near_g), cols_g)
     sum_in[...] = jnp.zeros_like(sum_in)
@@ -383,7 +441,8 @@
     lax.fori_loop(0, 8, back_block, 0)
     bias_sum = jnp.sum(sum_b[...].reshape(8, 32, 128), axis=0)
     bias_sum = jnp.sum(bias_sum, axis=1, keepdims=True)
-    pieces = gather_terms(sum_in[...], keep, gather) + gather_terms(sum_out[...], keep, gather)
+    pieces = gather_terms(sum_in[...], keep, gather[0], (0, 1, 2))
+    pieces += gather_terms(sum_out[...], keep, gather[1], (2, 1, 0))
     pieces.append(jnp.broadcast_to(bias_sum, (32, 20)))
 
     def share(buffer, mine, count, n, device):
@@ -425,7 +484,7 @@
 
     def finish(index, carry):
         depth, coil = index // 16, index % 16
-        both = stage[pl.ds(index, 128, stride=64), :].T
+        both = stage[pl.ds(index, 128, stride=64), :].astype(BF).T.astype(F32)
         part_of = weight[depth]
         for part in range(2):
             current = kv[part, coil, depth].astype(F32)
@@ -441,12 +500,15 @@
             pltpu.make_async_copy(kv.at[:, :, depth], out_hbm.at[:, :, depth], store_sem.at[depth])
         )
         stores[-1].start()
-    totals[...] = collect(second, 8, 10)
+    total = jnp.concatenate([collect(second, 8, 10) * norm] * 4, axis=0).T[:, :32]
+    grad_in[...] = total[:54]
+    grad_out[...] = total[54:108]
+    grad_bias[...] = total[108:109]
     for store in stores:
         store.wait()
 
 
-def run_cascade(*operands):
+def run_cascade(norm, *operands):
     blocks = pltpu.VMEM((128, 64, 128), BF)
     tile = pltpu.VMEM((2, 16, 4, 64, 128), BF)
     image = pltpu.VMEM((2, 64, 512), BF)
@@ -454,13 +516,15 @@
     table = pltpu.VMEM((1024, 1024), BF)
     hbm = pl.BlockSpec(memory_space=pl.ANY)
     return pl.pallas_call(
-        cascade,
+        functools.partial(cascade, norm),
         out_shape=(
             jax.ShapeDtypeStruct((2, 16, 4, 64, 128), BF),
-            jax.ShapeDtypeStruct((32, 128), F32),
+            jax.ShapeDtypeStruct((54, 32), F32),
+            jax.ShapeDtypeStruct((1, 32), F32),
+            jax.ShapeDtypeStruct((54, 32), F32),
         ),
-        in_specs=[hbm] * 6 + [VM] * 9,
-        out_specs=(hbm, VM),
+        in_specs=[hbm] * 9 + [VM] * 9,
+        out_specs=(hbm, VM, VM, VM),
         scratch_shapes=[
             tile, tile, tile,
             pltpu.VMEM((2, 1, 16, 64, 512), BF),
@@ -479,7 +543,15 @@
             pltpu.VMEM((256, 128), F32),
             pltpu.VMEM((16, 32, 128), F32),
             pltpu.VMEM((8, 32, 128), F32),
-            pltpu.SemaphoreType.DMA((6,)),
+            pltpu.VMEM((4, 64, 128), F32),
+            pltpu.VMEM((256, 128), F32),
+            pltpu.VMEM((256, 432), BF),
+            pltpu.VMEM((256, 432), BF),
+            pltpu.VMEM((144, 320), BF),
+            pltpu.VMEM((8, 54, 432), BF),
+            pltpu.VMEM((8, 54, 432), BF),
+            pltpu.VMEM((10, 54, 144), BF),
+            pltpu.SemaphoreType.DMA((9,)),
             pltpu.SemaphoreType.DMA((11,)),
             pltpu.SemaphoreType.DMA((11,)),
             pltpu.SemaphoreType.DMA((4,)),
@@ -500,33 +572,18 @@
     forward_y = jnp.asarray(forward_y_table(count_y, row_tile))
     inverse_z = jnp.asarray(z_table(count_z * depth_tile, True))
     forward_z = jnp.asarray(z_table(count_z * depth_tile, False))
-    spread = jnp.asarray(band_spread())
-    keep = jnp.asarray(band_keep())
-    gather = jnp.asarray(band_gather())
-    spread_out = jnp.asarray(out_spread())
-
-    flat_in = conv_in.transpose(0, 2, 3, 4, 1).reshape(32, 54)
-    w_in = jnp.einsum("ok,zkc->zoc", flat_in, spread).reshape(256, 432)
-    flat_back = conv_out[:, :, ::-1, ::-1, ::-1].transpose(1, 2, 3, 4, 0).reshape(32, 54)
-    w_back = jnp.einsum("ok,zkc->zoc", flat_back, spread).reshape(256, 432)
-    flat_out = conv_out.transpose(1, 2, 4, 0, 3).reshape(32, 54)
-    w_out = jnp.einsum("ik,qkr->rqi", flat_out, spread_out).reshape(144, 320)
-    bias = jnp.tile(bias_in, 8)[:, None]
-    weight = jnp.broadcast_to(
-        (step_size[0] * sample_mask.astype(F32))[:, :, None], (depth_tile, row_tile, x_cells)
+    norm = 1.0 / math.sqrt(x_cells * row_tile * count_y * depth_tile * count_z)
+    kspace_next, grad_in, grad_bias, grad_out = run_cascade(
+        norm, kspace, measured, cotangent, coil_field, inverse_y, forward_y,
+        jnp.asarray(band_spread()), jnp.asarray(band_spread_flipped()), jnp.asarray(out_spread()),
+        inverse_z, forward_z, sample_mask, step_size.reshape(1, 1),
+        conv_in.transpose(2, 3, 4, 1, 0).reshape(54, 32), bias_in.reshape(1, 32),
+        conv_out.transpose(2, 3, 4, 0, 1).reshape(54, 32),
+        jnp.asarray(band_keep()), jnp.asarray(band_gather()),
     )
-
-    kspace_next, totals = run_cascade(
-        kspace, measured, cotangent, coil_field, inverse_y, forward_y, inverse_z, forward_z,
-        weight, w_in, bias, w_out, w_back, keep, gather,
-    )
-
-    norm = 1.0 / math.sqrt(x_cells * row_tile * count_y * depth_tile * count_z)
-    totals = totals * norm
-    grad_in = totals[:, :54].reshape(32, 3, 3, 3, 2).transpose(0, 4, 1, 2, 3)
-    grad_out = totals[:, 54:108].reshape(32, 3, 3, 3, 2).transpose(4, 0, 1, 2, 3)
-    grad_out = grad_out[:, :, ::-1, ::-1, ::-1]
-    return kspace_next, grad_in, totals[:, 108], grad_out
+    grad_in = grad_in.reshape(3, 3, 3, 2, 32).transpose(4, 3, 0, 1, 2)
+    grad_out = grad_out.reshape(3, 3, 3, 2, 32).transpose(3, 4, 0, 1, 2)
+    return kspace_next, grad_in, grad_bias.reshape(32), grad_out
 
 
 def solution(mesh):

time: 161 us -> 132 us (0.82)
  Pallas kernels: 143 us -> 120 us
  matrix products: 4.21 us -> 0 us
    pallas_call x1, Pallas kernels: 143 us -> 120 us  [run_cascade(): pl.pallas_call(functools.partial(cascade, norm), out_shape=(jax.ShapeDtyp...]
    dot_general x3 -> x0, matrix products: 4.21 us -> none  [the longest x1 2 us: on_device(): w_in = jnp.einsum('ok,zkc->zoc', flat_in, spread).reshape(256, 432)]
    reshape x5 -> x4, local copies, waits for them, and re-layouts: 1.46 us -> 5.42 us  [the longest x1 1.37 us: on_device(): grad_in = grad_in.reshape(3, 3, 3, 2, 32).transpose(4, 3, 0, 1, 2)]
where the time goes in v3:
time: 132 us; the launch traced here: 131 us
  Pallas kernels  120 us (91%)
  local copies, waits for them, and re-layouts  9.12 us (7%)
    pallas_call x1, Pallas kernels, run_cascade(): pl.pallas_call(functools.partial(cascade, norm), out_shape=(jax.ShapeDtyp...  120 us
    unnamed x4, local copies, waits for them, and re-layouts  3.7 us

profile of v3, /device:TPU:1, one launch (start us, length us, event | category | flops | bytes accessed | tf_op | source)
XLA Modules:
  0.0 130.5 jit_solution(5067367782937986628)
XLA Ops:
  1.3 1.3 %reshape.30.flat_in = bf16[54,32]{1,0:T(8,128)(2,1)} reshape(bf16[3,3,3,2,32]{4,3,2,1,0:T(2,128)(2,1)} %bitcast.10) | data formatting | bytes 6912 | tf_op jit(solution)/shard_map/reshape | solution.py:580
  2.6 1.3 %reshape.32.flat_out = bf16[54,32]{1,0:T(8,128)(2,1)} reshape(bf16[3,3,3,2,32]{4,3,2,1,0:T(2,128)(2,1)} %bitcast.11) | data formatting | bytes 6912 | tf_op jit(solution)/shard_map/reshape | solution.py:581
  4.0 120.1 %cascade.1 = (bf16[2,16,4,64,128]{4,3,2,1,0:T(8,128)(2,1)}, f32[54,32]{1,0:T(8,128)}, f32[1,32]{1,0:T(1,128)}, f32[54,32]{1,0:T(8,128)}) custom-call(bf16[2,16,4,64,128]{4,3,2,1,0:T(8,128)(2,1)} %k_hbm.1, bf16[2,16,4,64,128]{4,3,2,1,0:T(8,128)(2,1)} %m_hbm.1, bf16[2,16,4,64,128]{4,3,2,1,0:T(8,128)(2,1)} %g_hbm.1, bf16[2,1,16,64,512]{4,3,2,1,0:T(8,128)(2,1)} %s_hbm.1, ...), custom_call_target="tpu_custom_call" | custom-call | tf_op jit(solution)/shard_map/cascade/pallas_call | solution.py:518
  124.1 1.4 %reshape.33 = f32[3,3,3,2,32]{4,3,2,1,0:T(2,128)} reshape(f32[54,32]{1,0:T(8,128)} %get-tuple-element.9) | data formatting | bytes 13824 | tf_op jit(solution)/shard_map/reshape | solution.py:584
  125.5 1.4 %reshape.35 = f32[3,3,3,2,32]{4,3,2,1,0:T(2,128)} reshape(f32[54,32]{1,0:T(8,128)} %get-tuple-element.11) | data formatting | bytes 13824 | tf_op jit(solution)/shard_map/reshape | solution.py:585
  126.8 0.0 copy-start
  126.8 3.2 %copy.25 = bf16[2,16,4,64,128]{4,3,2,1,0:T(8,128)(2,1)} copy(bf16[2,16,4,64,128]{4,3,2,1,0:T(8,128)(2,1)} %get-tuple-element.16) | data formatting | bytes 4194304
  130.0 0.0 copy-done
  130.0 0.5 copy.26
Async XLA Ops:
  126.8 3.2 %copy-start = (f32[1,32]{1,0:T(1,128)S(1)}, f32[1,32]{1,0:T(1,128)}, u32[]{:S(2)}) copy-start(f32[1,32]{1,0:T(1,128)} %get-tuple-element.10) | copy-start | bytes 388

commit v4 on v3

--- a/solution.py
+++ b/solution.py
@@ -91,7 +91,13 @@
     return as_bf16(spread.reshape(10, 54, 144))
 
 
-BATCH = 64
+AHEAD = 24
+ROWS = 4
+COILS = 2
+BESIDE = 16
+AFTER_IMAGE = AHEAD + 4 * ROWS + 8 * COILS
+CONV = 2
+BACK = 4
 
 
 def shifted(value, dy):
@@ -130,13 +136,13 @@
 
 def cascade(
     norm,
-    k_hbm, m_hbm, g_hbm, s_hbm, iy_hbm, fy_hbm, spread_in_hbm, spread_back_hbm, spread_out_hbm,
-    iz, fz, mask, step, flat_in, bias, flat_out, keep, gather,
-    out_hbm, grad_in, grad_bias, grad_out,
-    kv, gv, mv, sens, iy, fy, stage, sk, sg, sf, rk, rg, rf,
+    k_hbm, g_hbm, s_hbm, iy_hbm, fy_hbm, spread_in_hbm, spread_back_hbm, spread_out_hbm,
+    iz, fz, mask, step, taps_in, bias, taps_out, keep, gather,
+    out_hbm, weight, grad_in, grad_bias, grad_out,
+    kv, gv, sens, iy, fy, stage, sk, sg, sf, rk, rg, rf,
     own_k, own_g, near_k, near_g, q_mid, q_send, q_near,
     cols, cols_g, hidden, slope, sum_in, sum_out, sum_b, first, second,
-    weight, bias_cols, w_in, w_back, w_out, spread_in, spread_back, spread_out,
+    flat, bias_cols, w_in, w_back, w_out, spread_in, spread_back, spread_out,
     load_sem, send_sem, recv_sem, store_sem,
 ):
     my_y, my_z = lax.axis_index("gy"), lax.axis_index("gz")
@@ -150,7 +156,7 @@
     loads = [
         pltpu.make_async_copy(src, dst, load_sem.at[n])
         for n, (src, dst) in enumerate(
-            [(k_hbm, kv), (g_hbm, gv), (iy_hbm, iy), (s_hbm, sens), (fy_hbm, fy), (m_hbm, mv),
+            [(k_hbm, kv), (g_hbm, gv), (iy_hbm, iy), (s_hbm, sens), (fy_hbm, fy),
              (spread_in_hbm, spread_in), (spread_back_hbm, spread_back), (spread_out_hbm, spread_out)]
         )
     ]
@@ -194,31 +200,31 @@
         turn(kv, index)
         return carry
 
-    def send_k(i, carry):
-        t = target(i)
-        sk[t] = block_of(t)
-        remote(sk.at[t], rk.at[me], 0, t).start()
-        return carry
+    def half_of(t, half):
+        return stage[pl.ds(pl.multiple_of(t * 64 + half * 32, 32), 32), :].astype(BF)
 
     loads[0].wait()
-    lax.fori_loop(0, 64, turn_k, 0, unroll=2)
-    pl.semaphore_wait(barrier, 127)
-    rk[me] = block_of(me)
-    lax.fori_loop(1, 128, send_k, 0)
+    for half in range(2):
+        rows = pl.ds(half * 32, 32)
+
+        def send_k(i, carry):
+            t = target(i)
+            sk[t, rows] = half_of(t, half)
+            remote(sk.at[t, rows], rk.at[me, rows], 0, t).start()
+            return carry
+
+        lax.fori_loop(half * 32, half * 32 + 32, turn_k, 0, unroll=2)
+        if half == 0:
+            pl.semaphore_wait(barrier, 127)
+        rk[me, rows] = half_of(me, half)
+        lax.fori_loop(1, 128, send_k, 0)
 
     def turn_g(index, carry):
         turn(gv, index)
         return carry
 
-    def first_g(i, carry):
-        t = target(i)
-        sg[t] = block_of(t)
-        remote(sg.at[t], rg.at[me], 1, t).start()
-        return carry
-
     def keep_g(i, carry):
-        t = target(i)
-        sg[t] = block_of(t)
+        sg[i] = block_of(i)
         return carry
 
     def later_g(i, carry):
@@ -229,20 +235,24 @@
     loads[1].wait()
     lax.fori_loop(0, 64, turn_g, 0, unroll=2)
     rg[me] = block_of(me)
-    lax.fori_loop(1, BATCH, first_g, 0)
-    lax.fori_loop(BATCH, 128, keep_g, 0, unroll=2)
-
-    for n in (6, 7, 8):
+    lax.fori_loop(0, 128, keep_g, 0, unroll=4)
+    lax.fori_loop(1, AHEAD, later_g, 0)
+
+    for n in (5, 6, 7):
         loads[n].wait()
     contract = (((0,), (0,)), ((), ()))
+    for tap in range(27):
+        flat[0, pl.ds(tap * 2, 2), :] = taps_in[tap].astype(F32)
+        flat[1, pl.ds(tap * 2, 2), :] = taps_out[tap].astype(F32)
+    flat_in, flat_out = flat[0].astype(BF), flat[1].astype(BF)
     for zo in range(8):
         rows = pl.ds(zo * 32, 32)
-        band = lax.dot_general(flat_in[...], spread_in[zo], contract, preferred_element_type=F32)
+        band = lax.dot_general(flat_in, spread_in[zo], contract, preferred_element_type=F32)
         w_in[rows, :] = band.astype(BF)
-        band = lax.dot_general(flat_out[...], spread_back[zo], contract, preferred_element_type=F32)
+        band = lax.dot_general(flat_out, spread_back[zo], contract, preferred_element_type=F32)
         w_back[rows, :] = band.astype(BF)
     bands = [
-        lax.dot_general(spread_out[q], flat_out[...], contract, preferred_element_type=F32)
+        lax.dot_general(spread_out[q], flat_out, contract, preferred_element_type=F32)
         for q in range(10)
     ]
     w_out[...] = jnp.concatenate(bands, axis=1).astype(BF)
@@ -269,8 +279,13 @@
         every.wait_send()
         every.wait_recv()
 
-    def to_image(tiles, image):
+    def both_ways(up, down, near, n):
+        return [remote(up, near.at[0], n, right), remote(down, near.at[1], n + 1, left)]
+
+    def to_image(tiles, image, near, n, push):
         def rows(m, carry):
+            for i in range(ROWS):
+                push(AHEAD + m * ROWS + i, 0)
             lines = jnp.concatenate(
                 [tiles[pl.ds(gy * 16 + m * 4, 4)].reshape(256, 128) for gy in range(8)], axis=1
             )
@@ -287,6 +302,8 @@
 
             def coils(step_c, carry):
                 real, imag = carry
+                if chunk < COILS:
+                    push(AHEAD + 4 * ROWS + chunk * 8 + step_c, 0)
                 lines = []
                 for c in (2 * step_c, 2 * step_c + 1):
                     halves = [
@@ -306,32 +323,30 @@
 
             zero = jnp.zeros((64, 128), F32)
             real, imag = lax.fori_loop(0, 8, coils, (zero, zero), unroll=2)
-            image[0, :, lane] = real.astype(BF)
-            image[1, :, lane] = imag.astype(BF)
-
-    def to_neighbours(up, down, near, n):
-        copies = [remote(up, near.at[0], n, right), remote(down, near.at[1], n + 1, left)]
-        for copy in copies:
-            copy.start()
-        return copies
-
-    def beside(near, side, i):
-        inside = me > 0 if side == 0 else me < 127
-        return jnp.where(inside, near[side, i].astype(F32), 0.0)
+            image[chunk, 0] = real.astype(BF)
+            image[chunk, 1] = imag.astype(BF)
+            remote(image.at[chunk], near.at[0, chunk], n, right).start()
+            remote(image.at[chunk], near.at[1, chunk], n + 1, left).start()
+        return both_ways(image, image, near, n)
+
+    def inside(side, value):
+        return jnp.where(me > 0 if side == 0 else me < 127, value, 0.0)
+
+    def plane(image, i):
+        return jnp.concatenate([image[chunk, i] for chunk in range(4)], axis=1).astype(F32)
 
     def three(own, near):
         return (
-            lambda i: beside(near, 0, i),
-            lambda i: own[i].astype(F32),
-            lambda i: beside(near, 1, i),
+            lambda i: inside(0, plane(near.at[0], i)),
+            lambda i: plane(own, i),
+            lambda i: inside(1, plane(near.at[1], i)),
         )
 
     loads[2].wait()
     loads[3].wait()
     wait_blocks(sk, rk, 0)
-    to_image(rk, own_k)
-    copies = to_neighbours(own_k, own_k, near_k, 3)
-    lax.fori_loop(BATCH, 128, later_g, 0)
+    copies = to_image(rk, own_k, near_k, 3, later_g)
+    lax.fori_loop(AFTER_IMAGE, AFTER_IMAGE + BESIDE, later_g, 0)
     for copy in copies:
         copy.wait()
 
@@ -340,6 +355,8 @@
     hidden[pl.ds(65 * 32, 32), :] = jnp.zeros((32, 512), BF)
 
     def conv_in_block(zb, carry):
+        for i in range(CONV):
+            later_g(AFTER_IMAGE + BESIDE + zb * CONV + i, 0)
         window = cols[pl.ds(pl.multiple_of(zb * 144, 16), 432), :]
         pre = jnp.dot(w_in[...], window, preferred_element_type=F32)
         pre = pre + jnp.concatenate([bias_cols[...]] * 4, axis=1)
@@ -351,6 +368,8 @@
     lax.fori_loop(0, 8, conv_in_block, 0)
 
     def conv_out_block(zb, carry):
+        for i in range(CONV):
+            later_g(AFTER_IMAGE + BESIDE + 8 * CONV + zb * CONV + i, 0)
         window = hidden[pl.ds(pl.multiple_of(zb * 256, 256), 320), :]
         terms = jnp.dot(w_out[...], window, preferred_element_type=F32).reshape(18, 8, 512)
         rows = pl.ds(pl.multiple_of(zb * 8, 8), 8)
@@ -361,20 +380,23 @@
                 q_mid[dx, o, rows, :] = total
         return carry
 
-    lax.fori_loop(0, 8, conv_out_block, 0)
-    q_send[0] = q_mid[0].astype(BF)
-    q_send[1] = q_mid[2].astype(BF)
-    q_copies = to_neighbours(q_send.at[0], q_send.at[1], q_near, 5)
-
-    wait_blocks(sg, rg, 1)
-    to_image(rg, own_g)
-    g_copies = to_neighbours(own_g, own_g, near_g, 7)
-    for copy in q_copies:
+    for piece in range(4):
+        lax.fori_loop(piece * 2, piece * 2 + 2, conv_out_block, 0)
+        rows = pl.ds(piece * 16, 16)
+        q_send[0, piece] = q_mid[0, :, rows, :].astype(BF)
+        q_send[1, piece] = q_mid[2, :, rows, :].astype(BF)
+        remote(q_send.at[0, piece], q_near.at[0, piece], 5, right).start()
+        remote(q_send.at[1, piece], q_near.at[1, piece], 6, left).start()
+    lax.fori_loop(AFTER_IMAGE + BESIDE + 16 * CONV, 128, later_g, 0)
+    for copy in both_ways(q_send.at[0], q_send.at[1], q_near, 5):
         copy.wait()
 
-    for o in range(2):
-        total = beside(q_near, 0, o) + q_mid[1, o] + beside(q_near, 1, o)
-        q_mid[0, o] = total.astype(BF).astype(F32)
+    for piece in range(4):
+        rows = pl.ds(piece * 16, 16)
+        for o in range(2):
+            total = inside(0, q_near[0, piece, o].astype(F32)) + q_mid[1, o, rows, :]
+            total = total + inside(1, q_near[1, piece, o].astype(F32))
+            q_mid[0, o, rows, :] = total.astype(BF).astype(F32)
     for chunk in range(4):
         lane = pl.ds(chunk * 128, 128)
         r_r, r_i = q_mid[0, 0, :, lane], q_mid[0, 1, :, lane]
@@ -395,30 +417,28 @@
         lax.fori_loop(0, 8, spread, 0, unroll=2)
     loads[4].wait()
 
-    def send_f(step, carry):
-        m = (step + my_z // 4) % 4
+    def send_f(m, carry):
         lines = [stage[pl.ds(pl.multiple_of(lt * 1024 + m * 256, 256), 256), :] for lt in range(8)]
         lines = jnp.concatenate([part.astype(BF) for part in lines], axis=1)
         done = jnp.dot(lines, fy[...], preferred_element_type=F32).astype(BF)
         for gy in range(8):
             sf[pl.ds(gy * 16 + m * 4, 4)] = done[:, gy * 128 : gy * 128 + 128].reshape(4, 64, 128)
 
-        def start(j, inner):
-            t = (my_y + j % 8) % 8 * 16 + m * 4 + (my_z + j // 8) % 4
-
-            @pl.when(t != me)
-            def _():
-                remote(sf.at[t], rf.at[me], 2, t).start()
-
-            return inner
-
-        lax.fori_loop(0, 32, start, 0)
+        return carry
+
+    def start_f(i, carry):
+        t = target(i)
+        remote(sf.at[t], rf.at[me], 2, t).start()
         return carry
 
     lax.fori_loop(0, 4, send_f, 0)
     rf[me] = sf[me]
-
-    for copy in g_copies:
+    lax.fori_loop(1, AHEAD, start_f, 0)
+
+    wait_blocks(sg, rg, 1)
+    copies = to_image(rg, own_g, near_g, 7, start_f)
+    lax.fori_loop(AFTER_IMAGE, AFTER_IMAGE + BESIDE, start_f, 0)
+    for copy in copies:
         copy.wait()
     fill_columns(three(own_g, near_g), cols_g)
     sum_in[...] = jnp.zeros_like(sum_in)
@@ -427,6 +447,8 @@
     nt = (((1,), (1,)), ((), ()))
 
     def back_block(zb, carry):
+        for i in range(BACK):
+            start_f(AFTER_IMAGE + BESIDE + zb * BACK + i, 0)
         span = pl.ds(pl.multiple_of(zb * 144, 16), 432)
         window_g = cols_g[span, :]
         back = jnp.dot(w_back[...], window_g, preferred_element_type=F32)
@@ -439,6 +461,7 @@
         return carry
 
     lax.fori_loop(0, 8, back_block, 0)
+    lax.fori_loop(AFTER_IMAGE + BESIDE + 8 * BACK, 128, start_f, 0)
     bias_sum = jnp.sum(sum_b[...].reshape(8, 32, 128), axis=0)
     bias_sum = jnp.sum(bias_sum, axis=1, keepdims=True)
     pieces = gather_terms(sum_in[...], keep, gather[0], (0, 1, 2))
@@ -471,7 +494,6 @@
     first[my_z] = jnp.concatenate(pieces, axis=1)
     share(first, my_z, 16, 9, lambda to: my_y * 16 + to)
 
-    loads[5].wait()
     wait_blocks(sf, rf, 2)
 
     def widen(x, carry):
@@ -479,30 +501,26 @@
         return carry
 
     lax.fori_loop(0, 128, widen, 0, unroll=4)
-    second[my_y] = collect(first, 16, 9)
-    share(second, my_y, 8, 10, lambda to: to * 16 + my_z)
-
     def finish(index, carry):
-        depth, coil = index // 16, index % 16
-        both = stage[pl.ds(index, 128, stride=64), :].astype(BF).T.astype(F32)
-        part_of = weight[depth]
-        for part in range(2):
-            current = kv[part, coil, depth].astype(F32)
-            other = mv[part, coil, depth].astype(F32)
-            refine = both[part * 64 : part * 64 + 64]
-            kv[part, coil, depth] = (current - part_of * (current - other) + refine).astype(BF)
+        depth, coil = lax.div(index, 16), lax.rem(index, 16)
+        both = stage[pl.ds(index, 128, stride=64), :].astype(BF).T
+        kv[0, coil, depth], kv[1, coil, depth] = both[:64], both[64:]
         return carry
 
     stores = []
     for depth in range(4):
+        if depth == 2:
+            second[my_y] = collect(first, 16, 9)
+            share(second, my_y, 8, 10, lambda to: to * 16 + my_z)
         lax.fori_loop(depth * 16, depth * 16 + 16, finish, 0, unroll=2)
         stores.append(
             pltpu.make_async_copy(kv.at[:, :, depth], out_hbm.at[:, :, depth], store_sem.at[depth])
         )
         stores[-1].start()
     total = jnp.concatenate([collect(second, 8, 10) * norm] * 4, axis=0).T[:, :32]
-    grad_in[...] = total[:54]
-    grad_out[...] = total[54:108]
+    for tap in range(27):
+        grad_in[tap] = total[tap * 2 : tap * 2 + 2]
+        grad_out[tap] = total[54 + tap * 2 : 56 + tap * 2]
     grad_bias[...] = total[108:109]
     for store in stores:
         store.wait()
@@ -511,29 +529,31 @@
 def run_cascade(norm, *operands):
     blocks = pltpu.VMEM((128, 64, 128), BF)
     tile = pltpu.VMEM((2, 16, 4, 64, 128), BF)
-    image = pltpu.VMEM((2, 64, 512), BF)
-    near = pltpu.VMEM((2, 2, 64, 512), BF)
+    image = pltpu.VMEM((4, 2, 64, 128), BF)
+    near = pltpu.VMEM((2, 4, 2, 64, 128), BF)
+    pieces = pltpu.VMEM((2, 4, 2, 16, 512), BF)
     table = pltpu.VMEM((1024, 1024), BF)
     hbm = pl.BlockSpec(memory_space=pl.ANY)
     return pl.pallas_call(
         functools.partial(cascade, norm),
         out_shape=(
             jax.ShapeDtypeStruct((2, 16, 4, 64, 128), BF),
-            jax.ShapeDtypeStruct((54, 32), F32),
+            jax.ShapeDtypeStruct((4, 64, 128), F32),
+            jax.ShapeDtypeStruct((27, 2, 32), F32),
             jax.ShapeDtypeStruct((1, 32), F32),
-            jax.ShapeDtypeStruct((54, 32), F32),
+            jax.ShapeDtypeStruct((27, 2, 32), F32),
         ),
-        in_specs=[hbm] * 9 + [VM] * 9,
-        out_specs=(hbm, VM, VM, VM),
+        in_specs=[hbm] * 8 + [VM] * 9,
+        out_specs=(hbm, VM, VM, VM, VM),
         scratch_shapes=[
-            tile, tile, tile,
+            tile, tile,
             pltpu.VMEM((2, 1, 16, 64, 512), BF),
             table, table,
             pltpu.VMEM((8192, 128), F32),
             blocks, blocks, blocks, blocks, blocks, blocks,
             image, image, near, near,
             pltpu.VMEM((3, 2, 64, 512), F32),
-            near, near,
+            pieces, pieces,
             pltpu.VMEM((1440, 512), BF),
             pltpu.VMEM((1440, 512), BF),
             pltpu.VMEM((66 * 32, 512), BF),
@@ -543,7 +563,7 @@
             pltpu.VMEM((256, 128), F32),
             pltpu.VMEM((16, 32, 128), F32),
             pltpu.VMEM((8, 32, 128), F32),
-            pltpu.VMEM((4, 64, 128), F32),
+            pltpu.VMEM((2, 54, 32), F32),
             pltpu.VMEM((256, 128), F32),
             pltpu.VMEM((256, 432), BF),
             pltpu.VMEM((256, 432), BF),
@@ -551,7 +571,7 @@
             pltpu.VMEM((8, 54, 432), BF),
             pltpu.VMEM((8, 54, 432), BF),
             pltpu.VMEM((10, 54, 144), BF),
-            pltpu.SemaphoreType.DMA((9,)),
+            pltpu.SemaphoreType.DMA((8,)),
             pltpu.SemaphoreType.DMA((11,)),
             pltpu.SemaphoreType.DMA((11,)),
             pltpu.SemaphoreType.DMA((4,)),
@@ -573,14 +593,17 @@
     inverse_z = jnp.asarray(z_table(count_z * depth_tile, True))
     forward_z = jnp.asarray(z_table(count_z * depth_tile, False))
     norm = 1.0 / math.sqrt(x_cells * row_tile * count_y * depth_tile * count_z)
-    kspace_next, grad_in, grad_bias, grad_out = run_cascade(
-        norm, kspace, measured, cotangent, coil_field, inverse_y, forward_y,
+    refine, weight, grad_in, grad_bias, grad_out = run_cascade(
+        norm, kspace, cotangent, coil_field, inverse_y, forward_y,
         jnp.asarray(band_spread()), jnp.asarray(band_spread_flipped()), jnp.asarray(out_spread()),
         inverse_z, forward_z, sample_mask, step_size.reshape(1, 1),
-        conv_in.transpose(2, 3, 4, 1, 0).reshape(54, 32), bias_in.reshape(1, 32),
-        conv_out.transpose(2, 3, 4, 0, 1).reshape(54, 32),
+        conv_in.transpose(2, 3, 4, 1, 0).reshape(27, 2, 32), bias_in.reshape(1, 32),
+        conv_out.transpose(2, 3, 4, 0, 1).reshape(27, 2, 32),
         jnp.asarray(band_keep()), jnp.asarray(band_gather()),
     )
+    current = kspace.astype(F32)
+    kspace_next = current - weight * (current - measured.astype(F32)) + refine.astype(F32)
+    kspace_next = kspace_next.astype(BF)
     grad_in = grad_in.reshape(3, 3, 3, 2, 32).transpose(4, 3, 0, 1, 2)
     grad_out = grad_out.reshape(3, 3, 3, 2, 32).transpose(3, 4, 0, 1, 2)
     return kspace_next, grad_in, grad_bias.reshape(32), grad_out

time: 132 us -> 124 us (0.939)
  local copies, waits for them, and re-layouts: 9.12 us -> 1.75 us
  other arithmetic: 0 us -> 4.7 us
  Pallas kernels: 120 us -> 116 us
    reshape x4 -> x0, local copies, waits for them, and re-layouts: 5.42 us -> none  [the longest x1 1.37 us: on_device(): grad_in = grad_in.reshape(3, 3, 3, 2, 32).transpose(4, 3, 0, 1, 2)]
    convert_element_type x0 -> x1, other arithmetic: none -> 4.7 us  [on_device(): kspace_next = kspace_next.astype(BF)]
    pallas_call x1, Pallas kernels: 120 us -> 116 us  [run_cascade(): pl.pallas_call(functools.partial(cascade, norm), out_shape=(jax.ShapeDtyp...]
    unnamed x4 -> x13, local copies, waits for them, and re-layouts: 3.7 us -> 1.75 us
where the time goes in v4:
time: 124 us
  Pallas kernels  116 us (94%)
  other arithmetic  4.7 us (4%)
  local copies, waits for them, and re-layouts  1.75 us (1%)
  between operations  1.35 us (1%)
    pallas_call x1, Pallas kernels, run_cascade(): pl.pallas_call(functools.partial(cascade, norm), out_shape=(jax.ShapeDtyp...  116 us
    convert_element_type x1, other arithmetic, on_device(): kspace_next = kspace_next.astype(BF)  4.7 us

profile of v4, /device:TPU:1, one launch (start us, length us, event | category | flops | bytes accessed | tf_op | source)
XLA Modules:
  0.0 123.5 jit_solution(3109245679450082213)
XLA Ops:
  1.3 0.0 copy-start
  1.3 0.0 copy-start.1
  1.3 115.7 %cascade.1 = (bf16[2,16,4,64,128]{4,3,2,1,0:T(8,128)(2,1)}, f32[4,64,128]{2,1,0:T(8,128)}, f32[27,2,32]{2,1,0:T(2,128)}, f32[1,32]{1,0:T(1,128)}, f32[27,2,32]{2,1,0:T(2,128)}) custom-call(bf16[2,16,4,64,128]{4,3,2,1,0:T(8,128)(2,1)} %k_hbm.1, bf16[2,16,4,64,128]{4,3,2,1,0:T(8,128)(2,1)} %g_hbm.1, bf16[2,1,16,64,512]{4,3,2,1,0:T(8,128)(2,1)} %s_hbm.1, ...), custom_call_target="tpu_custom_call" | custom-call | tf_op jit(solution)/shard_map/cascade/pallas_call | solution.py:537
  117.0 0.0 copy-done
  117.0 0.0 copy-done.1
  117.1 0.0 copy-start.3
  117.1 0.0 copy-start.4
  117.1 0.0 copy-start.2
  117.1 4.7 %fusion.2 = bf16[2,16,4,64,128]{4,3,2,1,0:T(8,128)(2,1)} fusion(bf16[2,16,4,64,128]{4,3,2,1,0:T(8,128)(2,1)S(1)} %copy-done, bf16[2,16,4,64,128]{4,3,2,1,0:T(8,128)(2,1)} %get-tuple-element.10, bf16[2,16,4,64,128]{4,3,2,1,0:T(8,128)(2,1)S(1)} %copy-done.1, f32[4,64,128]{2,1,0:T(8,128)} %get-tuple-element.9), kind=kLoop, calls=%fused_computation.4 | loop fusion | flops 8388608 | bytes 8519680 | tf_op jit(solution)/shard_map/convert_element_type | solution.py:606
  121.8 0.0 copy-done.3
  121.8 0.6 copy.26
  122.4 0.0 copy-done.4
  122.4 0.5 copy.27
  122.9 0.0 copy-done.2
  122.9 0.6 copy.28
Async XLA Ops:
  1.3 115.8 %copy-start = (bf16[2,16,4,64,128]{4,3,2,1,0:T(8,128)(2,1)S(1)}, bf16[2,16,4,64,128]{4,3,2,1,0:T(8,128)(2,1)}, u32[]{:S(2)}) copy-start(bf16[2,16,4,64,128]{4,3,2,1,0:T(8,128)(2,1)} %k_hbm.1) | copy-start | bytes 6291460
  1.3 115.8 %copy-start.1 = (bf16[2,16,4,64,128]{4,3,2,1,0:T(8,128)(2,1)S(1)}, bf16[2,16,4,64,128]{4,3,2,1,0:T(8,128)(2,1)}, u32[]{:S(2)}) copy-start(bf16[2,16,4,64,128]{4,3,2,1,0:T(8,128)(2,1)} %param.19) | copy-start | bytes 6291460
  117.1 4.7 %copy-start.3 = (f32[27,2,32]{2,1,0:T(2,128)S(1)}, f32[27,2,32]{2,1,0:T(2,128)}, u32[]{:S(2)}) copy-start(f32[27,2,32]{2,1,0:T(2,128)} %get-tuple-element.11) | copy-start | bytes 20740
  117.1 5.3 %copy-start.4 = (f32[1,32]{1,0:T(1,128)S(1)}, f32[1,32]{1,0:T(1,128)}, u32[]{:S(2)}) copy-start(f32[1,32]{1,0:T(1,128)} %get-tuple-element.12) | copy-start | bytes 388
  117.1 5.8 %copy-start.2 = (f32[27,2,32]{2,1,0:T(2,128)S(1)}, f32[27,2,32]{2,1,0:T(2,128)}, u32[]{:S(2)}) copy-start(f32[27,2,32]{2,1,0:T(2,128)} %get-tuple-element.13) | copy-start | bytes 20740

commit v5 on v4

--- a/solution.py
+++ b/solution.py
@@ -95,7 +95,7 @@
 ROWS = 4
 COILS = 2
 BESIDE = 16
-AFTER_IMAGE = AHEAD + 4 * ROWS + 8 * COILS
+AFTER_IMAGE = AHEAD + ROWS + 8 * COILS
 CONV = 2
 BACK = 4
 
@@ -109,16 +109,18 @@
     return jnp.where(lane == 511, 0.0, pltpu.roll(value, 511, value.ndim - 1))
 
 
-def fill_columns(images, cols):
+def clear_columns(cols):
     cols[pl.ds(0, 144), :] = jnp.zeros((144, 512), BF)
     cols[pl.ds(1296, 144), :] = jnp.zeros((144, 512), BF)
-    for dx, image in enumerate(images):
-        parts = [image(i) for i in range(2)]
-        for dy in range(3):
-            pair = jnp.stack([shifted(part, dy).reshape(8, 8, 512) for part in parts], axis=1)
-            pair = pair.reshape(8, 16, 512).astype(BF)
-            for zb in range(8):
-                cols[pl.ds((zb + 1) * 144 + (dy * 3 + dx) * 16, 16), :] = pair[zb]
+
+
+def fill_columns(dx, image, cols):
+    parts = [image(i) for i in range(2)]
+    for dy in range(3):
+        pair = jnp.stack([shifted(part, dy).reshape(8, 8, 512) for part in parts], axis=1)
+        pair = pair.reshape(8, 16, 512).astype(BF)
+        for zb in range(8):
+            cols[pl.ds((zb + 1) * 144 + (dy * 3 + dx) * 16, 16), :] = pair[zb]
 
 
 def gather_terms(total, keep, gather, order):
@@ -188,6 +190,8 @@
         c = lax.rem(pos_c + lax.rem(n, 2), 2)
         return (lax.div(y, 2) * 4 + x) * 16 + lax.rem(y, 2) * 8 + z * 2 + c
 
+    nt = (((1,), (1,)), ((), ()))
+
     def turn(source, index):
         depth, coil = index // 16, index % 16
         both = jnp.concatenate([source[0, coil, depth], source[1, coil, depth]], axis=0)
@@ -210,10 +214,10 @@
         def send_k(i, carry):
             t = target(i)
             sk[t, rows] = half_of(t, half)
-            remote(sk.at[t, rows], rk.at[me, rows], 0, t).start()
+            remote(sk.at[t, rows], rk.at[me, rows], 11 * half, t).start()
             return carry
 
-        lax.fori_loop(half * 32, half * 32 + 32, turn_k, 0, unroll=2)
+        lax.fori_loop(half * 32, half * 32 + 32, turn_k, 0, unroll=4)
         if half == 0:
             pl.semaphore_wait(barrier, 127)
         rk[me, rows] = half_of(me, half)
@@ -233,7 +237,7 @@
         return carry
 
     loads[1].wait()
-    lax.fori_loop(0, 64, turn_g, 0, unroll=2)
+    lax.fori_loop(0, 64, turn_g, 0, unroll=4)
     rg[me] = block_of(me)
     lax.fori_loop(0, 128, keep_g, 0, unroll=4)
     lax.fori_loop(1, AHEAD, later_g, 0)
@@ -267,10 +271,10 @@
         row = mask[pl.ds(depth, 1), :].astype(F32) * step[...]
         weight[depth] = upright(jnp.concatenate([row, row], axis=1))[:64]
 
-    def wait_blocks(sent, got, n):
+    def wait_blocks(sent, got, n, rows=64):
         every = pltpu.make_async_remote_copy(
-            src_ref=sent.at[pl.ds(0, 127)],
-            dst_ref=got.at[pl.ds(0, 127)],
+            src_ref=sent.at[pl.ds(0, 127), pl.ds(0, rows)],
+            dst_ref=got.at[pl.ds(0, 127), pl.ds(0, rows)],
             send_sem=send_sem.at[n],
             recv_sem=recv_sem.at[n],
             device_id=pair(right),
@@ -282,20 +286,34 @@
     def both_ways(up, down, near, n):
         return [remote(up, near.at[0], n, right), remote(down, near.at[1], n + 1, left)]
 
-    def to_image(tiles, image, near, n, push):
-        def rows(m, carry):
-            for i in range(ROWS):
-                push(AHEAD + m * ROWS + i, 0)
-            lines = jnp.concatenate(
-                [tiles[pl.ds(gy * 16 + m * 4, 4)].reshape(256, 128) for gy in range(8)], axis=1
-            )
-            done = jnp.dot(lines, iy[...], preferred_element_type=F32)
-            for lt in range(8):
-                span = pl.ds(pl.multiple_of(lt * 1024 + m * 256, 256), 256)
-                stage[span, :] = done[:, lt * 128 : lt * 128 + 128]
-            return carry
-
-        lax.fori_loop(0, 4, rows, 0)
+    def to_image(tiles, image, near, n, push, *arrivals):
+        parts = len(arrivals)
+        depth = 64 // parts
+
+        for part, (sent, sem) in enumerate(arrivals):
+            wait_blocks(sent, tiles, sem, depth)
+
+            def rows(m, carry):
+                push(AHEAD + 4 // parts * part + m, 0)
+                lines = jnp.concatenate(
+                    [
+                        tiles[pl.ds(gy * 16 + m * 4 * parts, 4 * parts), pl.ds(part * depth, depth)]
+                        .reshape(256, 128)
+                        for gy in range(8)
+                    ],
+                    axis=1,
+                )
+                done = jnp.dot(lines, iy[...], preferred_element_type=F32)
+                done = done.reshape(4 * parts, depth, 1024)
+                for lt in range(8):
+                    for k in range(4 * parts):
+                        start = lt * 1024 + (m * 4 * parts + k) * 64 + part * depth
+                        stage[pl.ds(pl.multiple_of(start, 32), depth), :] = done[
+                            k, :, lt * 128 : lt * 128 + 128
+                        ]
+                return carry
+
+            lax.fori_loop(0, 4 // parts, rows, 0)
 
         for chunk in range(4):
             lane = pl.ds(chunk * 128, 128)
@@ -303,7 +321,7 @@
             def coils(step_c, carry):
                 real, imag = carry
                 if chunk < COILS:
-                    push(AHEAD + 4 * ROWS + chunk * 8 + step_c, 0)
+                    push(AHEAD + ROWS + chunk * 8 + step_c, 0)
                 lines = []
                 for c in (2 * step_c, 2 * step_c + 1):
                     halves = [
@@ -335,22 +353,18 @@
     def plane(image, i):
         return jnp.concatenate([image[chunk, i] for chunk in range(4)], axis=1).astype(F32)
 
-    def three(own, near):
-        return (
-            lambda i: inside(0, plane(near.at[0], i)),
-            lambda i: plane(own, i),
-            lambda i: inside(1, plane(near.at[1], i)),
-        )
+    def fill(own, near, copies, columns):
+        fill_columns(1, lambda i: plane(own, i), columns)
+        for side, copy in enumerate(copies):
+            copy.wait()
+            fill_columns(2 * side, lambda i: inside(side, plane(near.at[side], i)), columns)
 
     loads[2].wait()
     loads[3].wait()
-    wait_blocks(sk, rk, 0)
-    copies = to_image(rk, own_k, near_k, 3, later_g)
+    copies = to_image(rk, own_k, near_k, 3, later_g, (sk, 0), (sk, 11))
     lax.fori_loop(AFTER_IMAGE, AFTER_IMAGE + BESIDE, later_g, 0)
-    for copy in copies:
-        copy.wait()
-
-    fill_columns(three(own_k, near_k), cols)
+    clear_columns(cols)
+    fill(own_k, near_k, copies, cols)
     hidden[pl.ds(0, 32), :] = jnp.zeros((32, 512), BF)
     hidden[pl.ds(65 * 32, 32), :] = jnp.zeros((32, 512), BF)
 
@@ -365,7 +379,7 @@
         slope[pl.ds(pl.multiple_of(zb * 256, 256), 256), :] = sig * (1.0 + pre * (1.0 - sig))
         return carry
 
-    lax.fori_loop(0, 8, conv_in_block, 0)
+    lax.fori_loop(0, 8, conv_in_block, 0, unroll=2)
 
     def conv_out_block(zb, carry):
         for i in range(CONV):
@@ -435,17 +449,13 @@
     rf[me] = sf[me]
     lax.fori_loop(1, AHEAD, start_f, 0)
 
-    wait_blocks(sg, rg, 1)
-    copies = to_image(rg, own_g, near_g, 7, start_f)
+    copies = to_image(rg, own_g, near_g, 7, start_f, (sg, 1))
     lax.fori_loop(AFTER_IMAGE, AFTER_IMAGE + BESIDE, start_f, 0)
-    for copy in copies:
-        copy.wait()
-    fill_columns(three(own_g, near_g), cols_g)
+    clear_columns(cols_g)
+    fill(own_g, near_g, copies, cols_g)
     sum_in[...] = jnp.zeros_like(sum_in)
     sum_out[...] = jnp.zeros_like(sum_out)
     sum_b[...] = jnp.zeros_like(sum_b)
-    nt = (((1,), (1,)), ((), ()))
-
     def back_block(zb, carry):
         for i in range(BACK):
             start_f(AFTER_IMAGE + BESIDE + zb * BACK + i, 0)
@@ -460,7 +470,7 @@
         sum_b[...] += wide[:, :128] + wide[:, 128:256] + wide[:, 256:384] + wide[:, 384:]
         return carry
 
-    lax.fori_loop(0, 8, back_block, 0)
+    lax.fori_loop(0, 8, back_block, 0, unroll=2)
     lax.fori_loop(AFTER_IMAGE + BESIDE + 8 * BACK, 128, start_f, 0)
     bias_sum = jnp.sum(sum_b[...].reshape(8, 32, 128), axis=0)
     bias_sum = jnp.sum(bias_sum, axis=1, keepdims=True)
@@ -496,6 +506,9 @@
 
     wait_blocks(sf, rf, 2)
 
+    second[my_y] = collect(first, 16, 9)
+    share(second, my_y, 8, 10, lambda to: to * 16 + my_z)
+
     def widen(x, carry):
         stage[pl.ds(pl.multiple_of(x * 64, 64), 64), :] = rf[x].astype(F32)
         return carry
@@ -509,10 +522,7 @@
 
     stores = []
     for depth in range(4):
-        if depth == 2:
-            second[my_y] = collect(first, 16, 9)
-            share(second, my_y, 8, 10, lambda to: to * 16 + my_z)
-        lax.fori_loop(depth * 16, depth * 16 + 16, finish, 0, unroll=2)
+        lax.fori_loop(depth * 16, depth * 16 + 16, finish, 0, unroll=4)
         stores.append(
             pltpu.make_async_copy(kv.at[:, :, depth], out_hbm.at[:, :, depth], store_sem.at[depth])
         )
@@ -572,8 +582,8 @@
             pltpu.VMEM((8, 54, 432), BF),
             pltpu.VMEM((10, 54, 144), BF),
             pltpu.SemaphoreType.DMA((8,)),
-            pltpu.SemaphoreType.DMA((11,)),
-            pltpu.SemaphoreType.DMA((11,)),
+            pltpu.SemaphoreType.DMA((12,)),
+            pltpu.SemaphoreType.DMA((12,)),
             pltpu.SemaphoreType.DMA((4,)),
         ],
         compiler_params=pltpu.CompilerParams(

time: 124 us -> 120 us (0.968)
  Pallas kernels: 116 us -> 112 us
    pallas_call x1, Pallas kernels: 116 us -> 112 us  [run_cascade(): pl.pallas_call(functools.partial(cascade, norm), out_shape=(jax.ShapeDtyp...]
where the time goes in v5:
time: 120 us; the launch traced here: 119 us
  Pallas kernels  112 us (93%)
  other arithmetic  4.7 us (4%)
  local copies, waits for them, and re-layouts  1.75 us (1%)
  between operations  1.35 us (1%)
    pallas_call x1, Pallas kernels, run_cascade(): pl.pallas_call(functools.partial(cascade, norm), out_shape=(jax.ShapeDtyp...  112 us
    convert_element_type x1, other arithmetic, on_device(): kspace_next = kspace_next.astype(BF)  4.7 us

profile of v5, /device:TPU:1, one launch (start us, length us, event | category | flops | bytes accessed | tf_op | source)
XLA Modules:
  0.0 119.4 jit_solution(10572738823792784961)
XLA Ops:
  1.3 0.0 copy-start
  1.3 0.0 copy-start.1
  1.3 111.6 %cascade.1 = (bf16[2,16,4,64,128]{4,3,2,1,0:T(8,128)(2,1)}, f32[4,64,128]{2,1,0:T(8,128)}, f32[27,2,32]{2,1,0:T(2,128)}, f32[1,32]{1,0:T(1,128)}, f32[27,2,32]{2,1,0:T(2,128)}) custom-call(bf16[2,16,4,64,128]{4,3,2,1,0:T(8,128)(2,1)} %k_hbm.1, bf16[2,16,4,64,128]{4,3,2,1,0:T(8,128)(2,1)} %g_hbm.1, bf16[2,1,16,64,512]{4,3,2,1,0:T(8,128)(2,1)} %s_hbm.1, ...), custom_call_target="tpu_custom_call" | custom-call | tf_op jit(solution)/shard_map/cascade/pallas_call | solution.py:547
  112.9 0.0 copy-done
  112.9 0.0 copy-done.1
  112.9 0.0 copy-start.3
  112.9 0.0 copy-start.4
  112.9 0.0 copy-start.2
  112.9 4.7 %fusion.2 = bf16[2,16,4,64,128]{4,3,2,1,0:T(8,128)(2,1)} fusion(bf16[2,16,4,64,128]{4,3,2,1,0:T(8,128)(2,1)S(1)} %copy-done, bf16[2,16,4,64,128]{4,3,2,1,0:T(8,128)(2,1)} %get-tuple-element.10, bf16[2,16,4,64,128]{4,3,2,1,0:T(8,128)(2,1)S(1)} %copy-done.1, f32[4,64,128]{2,1,0:T(8,128)} %get-tuple-element.9), kind=kLoop, calls=%fused_computation.4 | loop fusion | flops 8388608 | bytes 8519680 | tf_op jit(solution)/shard_map/convert_element_type | solution.py:616
  117.6 0.0 copy-done.3
  117.6 0.6 copy.26
  118.3 0.0 copy-done.4
  118.3 0.5 copy.27
  118.8 0.0 copy-done.2
  118.8 0.6 copy.28
Async XLA Ops:
  1.3 111.6 %copy-start = (bf16[2,16,4,64,128]{4,3,2,1,0:T(8,128)(2,1)S(1)}, bf16[2,16,4,64,128]{4,3,2,1,0:T(8,128)(2,1)}, u32[]{:S(2)}) copy-start(bf16[2,16,4,64,128]{4,3,2,1,0:T(8,128)(2,1)} %k_hbm.1) | copy-start | bytes 6291460
  1.3 111.6 %copy-start.1 = (bf16[2,16,4,64,128]{4,3,2,1,0:T(8,128)(2,1)S(1)}, bf16[2,16,4,64,128]{4,3,2,1,0:T(8,128)(2,1)}, u32[]{:S(2)}) copy-start(bf16[2,16,4,64,128]{4,3,2,1,0:T(8,128)(2,1)} %param.19) | copy-start | bytes 6291460
  112.9 4.7 %copy-start.3 = (f32[27,2,32]{2,1,0:T(2,128)S(1)}, f32[27,2,32]{2,1,0:T(2,128)}, u32[]{:S(2)}) copy-start(f32[27,2,32]{2,1,0:T(2,128)} %get-tuple-element.11) | copy-start | bytes 20740
  112.9 5.3 %copy-start.4 = (f32[1,32]{1,0:T(1,128)S(1)}, f32[1,32]{1,0:T(1,128)}, u32[]{:S(2)}) copy-start(f32[1,32]{1,0:T(1,128)} %get-tuple-element.12) | copy-start | bytes 388
  112.9 5.8 %copy-start.2 = (f32[27,2,32]{2,1,0:T(2,128)S(1)}, f32[27,2,32]{2,1,0:T(2,128)}, u32[]{:S(2)}) copy-start(f32[27,2,32]{2,1,0:T(2,128)} %get-tuple-element.13) | copy-start | bytes 20740

commit v6 on v5

--- a/solution.py
+++ b/solution.py
@@ -170,7 +170,7 @@
         pl.semaphore_signal(barrier, inc=1, device_id=pair(lax.rem(me + n, 128)), device_id_type=MESH)
         return carry
 
-    lax.fori_loop(1, 128, greet, 0)
+    lax.fori_loop(1, 128, greet, 0, unroll=4)
 
     def remote(src, dst, n, t):
         return pltpu.make_async_remote_copy(
@@ -221,7 +221,7 @@
         if half == 0:
             pl.semaphore_wait(barrier, 127)
         rk[me, rows] = half_of(me, half)
-        lax.fori_loop(1, 128, send_k, 0)
+        lax.fori_loop(1, 128, send_k, 0, unroll=2)
 
     def turn_g(index, carry):
         turn(gv, index)
@@ -340,7 +340,7 @@
                 return real, imag
 
             zero = jnp.zeros((64, 128), F32)
-            real, imag = lax.fori_loop(0, 8, coils, (zero, zero), unroll=2)
+            real, imag = lax.fori_loop(0, 8, coils, (zero, zero), unroll=4)
             image[chunk, 0] = real.astype(BF)
             image[chunk, 1] = imag.astype(BF)
             remote(image.at[chunk], near.at[0, chunk], n, right).start()
@@ -395,7 +395,7 @@
         return carry
 
     for piece in range(4):
-        lax.fori_loop(piece * 2, piece * 2 + 2, conv_out_block, 0)
+        lax.fori_loop(piece * 2, piece * 2 + 2, conv_out_block, 0, unroll=2)
         rows = pl.ds(piece * 16, 16)
         q_send[0, piece] = q_mid[0, :, rows, :].astype(BF)
         q_send[1, piece] = q_mid[2, :, rows, :].astype(BF)
@@ -428,7 +428,7 @@
                     stage[rows, :] = done[p * 64 : p * 64 + 64, k * 128 : k * 128 + 128]
             return carry
 
-        lax.fori_loop(0, 8, spread, 0, unroll=2)
+        lax.fori_loop(0, 8, spread, 0, unroll=4)
     loads[4].wait()
 
     def send_f(m, carry):
@@ -445,7 +445,7 @@
         remote(sf.at[t], rf.at[me], 2, t).start()
         return carry
 
-    lax.fori_loop(0, 4, send_f, 0)
+    lax.fori_loop(0, 4, send_f, 0, unroll=2)
     rf[me] = sf[me]
     lax.fori_loop(1, AHEAD, start_f, 0)
 
@@ -513,7 +513,7 @@
         stage[pl.ds(pl.multiple_of(x * 64, 64), 64), :] = rf[x].astype(F32)
         return carry
 
-    lax.fori_loop(0, 128, widen, 0, unroll=4)
+    lax.fori_loop(0, 128, widen, 0, unroll=8)
     def finish(index, carry):
         depth, coil = lax.div(index, 16), lax.rem(index, 16)
         both = stage[pl.ds(index, 128, stride=64), :].astype(BF).T

time: 120 us -> 119 us (level)
  no operation moved by 1% of the time
where the time goes in v6:
time: 119 us
  Pallas kernels  111 us (93%)
  other arithmetic  4.7 us (4%)
  local copies, waits for them, and re-layouts  1.75 us (1%)
  between operations  1.35 us (1%)
    pallas_call x1, Pallas kernels, run_cascade(): pl.pallas_call(functools.partial(cascade, norm), out_shape=(jax.ShapeDtyp...  111 us
    convert_element_type x1, other arithmetic, on_device(): kspace_next = kspace_next.astype(BF)  4.7 us

profile of v6, /device:TPU:1, one launch (start us, length us, event | category | flops | bytes accessed | tf_op | source)
XLA Modules:
  0.0 118.6 jit_solution(15821638562543859253)
XLA Ops:
  1.3 0.0 copy-start
  1.3 0.0 copy-start.1
  1.3 110.8 %cascade.1 = (bf16[2,16,4,64,128]{4,3,2,1,0:T(8,128)(2,1)}, f32[4,64,128]{2,1,0:T(8,128)}, f32[27,2,32]{2,1,0:T(2,128)}, f32[1,32]{1,0:T(1,128)}, f32[27,2,32]{2,1,0:T(2,128)}) custom-call(bf16[2,16,4,64,128]{4,3,2,1,0:T(8,128)(2,1)} %k_hbm.1, bf16[2,16,4,64,128]{4,3,2,1,0:T(8,128)(2,1)} %g_hbm.1, bf16[2,1,16,64,512]{4,3,2,1,0:T(8,128)(2,1)} %s_hbm.1, ...), custom_call_target="tpu_custom_call" | custom-call | tf_op jit(solution)/shard_map/cascade/pallas_call | solution.py:547
  112.1 0.0 copy-done
  112.1 0.0 copy-done.1
  112.2 0.0 copy-start.3
  112.2 0.0 copy-start.4
  112.2 0.0 copy-start.2
  112.2 4.7 %fusion.2 = bf16[2,16,4,64,128]{4,3,2,1,0:T(8,128)(2,1)} fusion(bf16[2,16,4,64,128]{4,3,2,1,0:T(8,128)(2,1)S(1)} %copy-done, bf16[2,16,4,64,128]{4,3,2,1,0:T(8,128)(2,1)} %get-tuple-element.10, bf16[2,16,4,64,128]{4,3,2,1,0:T(8,128)(2,1)S(1)} %copy-done.1, f32[4,64,128]{2,1,0:T(8,128)} %get-tuple-element.9), kind=kLoop, calls=%fused_computation.4 | loop fusion | flops 8388608 | bytes 8519680 | tf_op jit(solution)/shard_map/convert_element_type | solution.py:616
  116.9 0.0 copy-done.3
  116.9 0.6 copy.26
  117.5 0.0 copy-done.4
  117.5 0.5 copy.27
  118.0 0.0 copy-done.2
  118.0 0.6 copy.28
Async XLA Ops:
  1.3 110.9 %copy-start = (bf16[2,16,4,64,128]{4,3,2,1,0:T(8,128)(2,1)S(1)}, bf16[2,16,4,64,128]{4,3,2,1,0:T(8,128)(2,1)}, u32[]{:S(2)}) copy-start(bf16[2,16,4,64,128]{4,3,2,1,0:T(8,128)(2,1)} %k_hbm.1) | copy-start | bytes 6291460
  1.3 110.9 %copy-start.1 = (bf16[2,16,4,64,128]{4,3,2,1,0:T(8,128)(2,1)S(1)}, bf16[2,16,4,64,128]{4,3,2,1,0:T(8,128)(2,1)}, u32[]{:S(2)}) copy-start(bf16[2,16,4,64,128]{4,3,2,1,0:T(8,128)(2,1)} %param.19) | copy-start | bytes 6291460
  112.2 4.7 %copy-start.3 = (f32[27,2,32]{2,1,0:T(2,128)S(1)}, f32[27,2,32]{2,1,0:T(2,128)}, u32[]{:S(2)}) copy-start(f32[27,2,32]{2,1,0:T(2,128)} %get-tuple-element.11) | copy-start | bytes 20740
  112.2 5.3 %copy-start.4 = (f32[1,32]{1,0:T(1,128)S(1)}, f32[1,32]{1,0:T(1,128)}, u32[]{:S(2)}) copy-start(f32[1,32]{1,0:T(1,128)} %get-tuple-element.12) | copy-start | bytes 388
  112.2 5.8 %copy-start.2 = (f32[27,2,32]{2,1,0:T(2,128)S(1)}, f32[27,2,32]{2,1,0:T(2,128)}, u32[]{:S(2)}) copy-start(f32[27,2,32]{2,1,0:T(2,128)} %get-tuple-element.13) | copy-start | bytes 20740
